TPU v7x, 256 devices: a whole 4x4x8 slice. The times are simulated.
256 devices in a mesh: src: 8 (over z), space: 32 (over x, y, core).
Axes of the slice: x: 4, y: 4, z: 8, core: 2. Of those that a mesh axis runs over, the one named last changes fastest.
Arguments:
- background: float32 [2, 8, 3, 64, 32, 128], P(None, 'src', None, 'space'), may hold values from -6 to 6
- warm_start: float32 [2, 8, 3, 64, 32, 128], P(None, 'src', None, 'space'), may hold values from -0.15625 to 0.15625
- conductivity: float32 [64, 32, 128], P('space'), may hold values from 0.3 to 3
- frequencies: float32 [8], replicated, may hold values from 0.1 to 1
- pair_freq: int32 [8], P('src'), may hold values from 0 to 7
- weighted_residual: float32 [2, 8, 4096], P(None, 'src', 'space'), may hold values from -6 to 6
- datum_layer_index: int32 [4096, 1], replicated, may hold values from 0 to 31; in each aligned block of 128 rows (0 to 127, 128 to 255, ...) at most 8 rows name the same one
- receiver_flat_cell: int32 [4096], replicated, may hold values from 0 to 8191
- receiver_component: int32 [4096], replicated, may hold values from 0 to 2
Outputs:
- adjoint: float32 [2, 8, 3, 64, 32, 128], P(None, 'src', None, 'space')
- gradient: float32 [64, 32, 128], P('space', 'src')
Inputs may be any that keep to these rules, and one draw needn't show every extreme that they name: `datum_layer_index`: among the 128 measurements of each aligned block (the measurements of one device), no slab is named by more than 8 of them, a bound that some block reaches.
All inputs are finite; a program needn't handle non-finite values.
Results may differ from a plain program's by a relative error of at most 0.0001.
Values sent between devices are 32-bit elements; how exact they have to be, the bound alone decides.
No kernel may reach another device: no remote copies, remote signals or barrier semaphores. Data moves between devices by JAX's collectives and lax.ppermute only.
A program may use at most 64 MiB of HBM per device.

v0:
```python
import jax
import jax.numpy as jnp
from jax import lax
from jax.sharding import PartitionSpec as P

ITERS = 4


def from_behind(block, axis, distance):
    devices = range(lax.axis_size(axis))
    route = [(i - distance, i) for i in devices if i - distance in devices]
    return lax.ppermute(block, axis, route)


def diff_forward(field, spatial):
    base = field[..., :-1, :-1, :-1]
    if spatial == 0:
        return field[..., 1:, :-1, :-1] - base
    if spatial == 1:
        return field[..., :-1, 1:, :-1] - base
    return field[..., :-1, :-1, 1:] - base


def diff_backward(field, spatial):
    base = field[..., 1:, 1:, 1:]
    if spatial == 0:
        return base - field[..., :-1, 1:, 1:]
    if spatial == 1:
        return base - field[..., 1:, :-1, 1:]
    return base - field[..., 1:, 1:, :-1]


def curl_forward(padded):
    comp_x = padded[..., 0, :, :, :]
    comp_y = padded[..., 1, :, :, :]
    comp_z = padded[..., 2, :, :, :]
    mag_x = diff_forward(comp_z, 1) - diff_forward(comp_y, 2)
    mag_y = diff_forward(comp_x, 2) - diff_forward(comp_z, 0)
    mag_z = diff_forward(comp_y, 0) - diff_forward(comp_x, 1)
    return jnp.stack([mag_x, mag_y, mag_z], axis=-4)


def curl_backward(magnetic):
    mag_x = magnetic[..., 0, :, :, :]
    mag_y = magnetic[..., 1, :, :, :]
    mag_z = magnetic[..., 2, :, :, :]
    out_x = diff_backward(mag_z, 1) - diff_backward(mag_y, 2)
    out_y = diff_backward(mag_x, 2) - diff_backward(mag_z, 0)
    out_z = diff_backward(mag_y, 0) - diff_backward(mag_x, 1)
    return jnp.stack([out_x, out_y, out_z], axis=-4)


def pad_sides(field):
    return jnp.pad(field, ((0, 0), (0, 0), (0, 0), (0, 0), (1, 1), (1, 1)))


def curl_curl(field, measurement_position):
    upper = from_behind(field[:, :, :, 0:1], "space", -1)
    extended = jnp.concatenate([jnp.zeros_like(upper), field, upper], axis=3)
    magnetic = curl_forward(pad_sides(extended))
    lower = from_behind(magnetic[:, :, :, -1:], "space", 1)
    first_plane = jnp.where(measurement_position == 0, magnetic[:, :, :, 0:1], lower)
    magnetic = jnp.concatenate([first_plane, magnetic[:, :, :, 1:]], axis=3)
    return curl_backward(magnetic)


def inner(first_vec, second_vec):
    real_part = jnp.sum(
        first_vec[0] * second_vec[0] + first_vec[1] * second_vec[1], axis=(1, 2, 3, 4)
    )
    quadrature_share = jnp.sum(
        first_vec[0] * second_vec[1] - first_vec[1] * second_vec[0], axis=(1, 2, 3, 4)
    )
    return (real_part, quadrature_share)


def squared(field):
    return jnp.sum(field[0] * field[0] + field[1] * field[1], axis=(1, 2, 3, 4))


def scaled(coef_re, coef_im, field):
    part_re = coef_re[:, None, None, None, None]
    part_im = coef_im[:, None, None, None, None]
    return jnp.stack(
        [part_re * field[0] - part_im * field[1], part_re * field[1] + part_im * field[0]]
    )


def shards(
    background,
    warm_start,
    conductivity,
    frequencies,
    pair_freq,
    weighted_residual,
    datum_layer_index,
    receiver_flat_cell,
    receiver_component,
):
    slab_partition = lax.axis_size("space")
    measurement_position = lax.axis_index("space")
    pair_count = background.shape[1]
    planes, rows_y, rows_z = (background.shape[3], background.shape[4], background.shape[5])
    slab_cells = planes * rows_y * rows_z
    local_measurements = weighted_residual.shape[2]
    slab_limit = 2 * local_measurements // slab_partition
    owning_slab = datum_layer_index[:, 0]
    holding_slab = lax.dynamic_slice_in_dim(
        owning_slab, measurement_position * local_measurements, local_measurements
    )
    one_hot = (
        holding_slab[:, None] == jnp.arange(slab_partition, dtype=jnp.int32)[None, :]
    ).astype(jnp.int32)
    rank_in = jnp.sum(jnp.cumsum(one_hot, axis=0) * one_hot, axis=1) - 1
    target_layer_slot = holding_slab * slab_limit + rank_in
    outgoing = (
        jnp.zeros((2, pair_count, slab_partition * slab_limit), jnp.float32)
        .at[:, :, target_layer_slot]
        .set(weighted_residual)
    )
    incoming = lax.all_to_all(outgoing, "space", split_axis=2, concat_axis=2, tiled=True)
    slab_blocks = owning_slab.reshape(slab_partition, local_measurements)
    is_mine = (slab_blocks == measurement_position).astype(jnp.int32)
    slot_index = (
        jnp.cumsum(is_mine, axis=1)
        - 1
        + jnp.arange(slab_partition, dtype=jnp.int32)[:, None] * slab_limit
    )
    slot_index = jnp.where(is_mine > 0, slot_index, 0).reshape(-1)
    values = incoming[:, :, slot_index] * is_mine.reshape(-1).astype(jnp.float32)
    target = receiver_component * slab_cells + receiver_flat_cell
    flat_src = jnp.zeros((2, pair_count, 3 * slab_cells), jnp.float32).at[:, :, target].add(values)
    source = flat_src.reshape(2, pair_count, 3, planes, rows_y, rows_z)
    freq_hot = (
        pair_freq[:, None] == jnp.arange(frequencies.shape[0], dtype=jnp.int32)[None, :]
    ).astype(jnp.float32)
    wave_k = jnp.sum(freq_hot * frequencies[None, :], axis=1)
    damping = wave_k[:, None, None, None, None] * conductivity[None, None]

    def operate(field):
        curled = curl_curl(field, measurement_position)
        return jnp.stack([curled[0] - damping * field[1], curled[1] + damping * field[0]])

    adjoint = warm_start
    residual = source - operate(adjoint)
    direction = residual
    mapped = operate(direction)
    for sweep in range(ITERS):
        mixed_product_real, cross_im = inner(mapped, residual)
        mixed_product_real, cross_im, projected_magnitude = lax.psum(
            (mixed_product_real, cross_im, squared(mapped)), "space"
        )
        alpha_re = mixed_product_real / projected_magnitude
        alpha_im = cross_im / projected_magnitude
        adjoint = adjoint + scaled(alpha_re, alpha_im, direction)
        residual = residual - scaled(alpha_re, alpha_im, mapped)
        if sweep + 1 < ITERS:
            fresh = operate(residual)
            turn_re, turn_im = lax.psum(inner(mapped, fresh), "space")
            beta_re = -turn_re / projected_magnitude
            beta_im = -turn_im / projected_magnitude
            direction = residual + scaled(beta_re, beta_im, direction)
            mapped = fresh + scaled(beta_re, beta_im, mapped)
    weights = wave_k[:, None, None, None, None]
    local_terms = jnp.sum(
        weights * (adjoint[0] * background[1] + adjoint[1] * background[0]), axis=(0, 1)
    )
    gradient = lax.psum_scatter(local_terms, "src", scatter_dimension=1, tiled=True)
    return (adjoint, gradient)


def solution(mesh):
    placed = (
        P(None, "src", None, "space", None, None),
        P(None, "src", None, "space", None, None),
        P("space", None, None),
        P(),
        P("src"),
        P(None, "src", "space"),
        P(),
        P(),
        P(),
    )
    return jax.shard_map(
        shards,
        mesh=mesh,
        in_specs=placed,
        out_specs=(P(None, "src", None, "space", None, None), P("space", "src", None)),
        check_vma=False,
    )
```

profile of v0, /device:TPU:1, one launch (start us, length us, event | category | flops | bytes accessed | tf_op | source)
XLA Modules:
  0.0 618.6 jit_solution(10655991864128447970)
XLA Ops:
  0.6 0.7 fusion.165
  1.7 0.7 fusion.164
  2.4 0.8 copy.53
  3.2 1.5 scatter_custom_fusion
  4.7 8.6 %all-to-all-start = ((f32[2,1,256]{0,1,2:T(1,128)}), f32[2,1,256]{0,1,2:T(1,128)S(1)}, u32[]{:S(2)}, u32[]{:S(2)}) async-start(f32[2,1,256]{0,1,2:T(1,128)} %bitcast.8), calls=%async_computation | async-start | bytes 262144 | tf_op jit(solution)/shard_map/all_to_all | solution.py:121
  13.3 0.9 slice.816
  14.2 2.1 collective-permute-start
  16.3 0.7 fusion.169
  18.2 0.7 compare_select_fusion.2
  18.9 1.3 fusion.163
  20.5 1.0 pad_maximum_fusion.5
  22.2 3.1 collective-permute-start.1
  25.3 0.6 broadcast_multiply_fusion
  25.9 40.5 %scatter_custom_fusion.1 = f32[2,24576]{0,1:T(8,128)} fusion(s32[4096]{0:T(1024)S(1)} %get-tuple-element.139, f32[]{:T(128)} %constant.13.clone.1, f32[4096]{0:T(1024)S(1)} %bitcast.519, f32[2,256]{0,1:T(8,128)S(1)} %bitcast.517, s32[4096]{0:T(1024)S(1)} %get-tuple-element.140), kind=kCustom, calls=%fused_computation.3 | custom fusion | flops 16384 | bytes 360452 | tf_op jit(solution)/shard_map/scatter-add | solution.py:132
  66.4 7.6 %copy.61 = f32[2,1,3,2,32,128]{5,4,3,0,2,1:T(8,128)S(1)} copy(f32[2,1,3,2,32,128]{0,5,4,3,2,1:T(8,128)} %bitcast.516) | data formatting | bytes 393216 | tf_op jit(solution)/shard_map/reshape | solution.py:133
  75.0 1.9 collective-permute-start.2
  77.0 4.0 collective-permute-done.2
  81.7 1.9 collective-permute-start.3
  83.7 3.1 collective-permute-done.3
  87.1 0.7 fusion.127
  87.7 64.5 %all-reduce.12 = (f32[1]{0:T(128)}, f32[1]{0:T(128)}, f32[1]{0:T(128)}) all-reduce(f32[1]{0:T(128)} %bitcast.53, f32[1]{0:T(128)} %bitcast.50, f32[1]{0:T(128)} %bitcast.49), channel_id=1, replica_groups=mesh['src'=8,'space'=32] {'space'}, use_global_device_ids=true, to_apply=%region_11.12 | all-reduce | flops 3 | bytes 24 | tf_op jit(solution)/shard_map/psum | solution.py:150
  155.2 2.9 collective-permute-start.4
  158.1 3.0 collective-permute-done.4
  161.8 1.9 collective-permute-start.5
  163.8 3.1 collective-permute-done.5
  167.2 0.7 add_reduce_fusion.1
  167.9 61.0 %all-reduce.11 = (f32[1]{0:T(128)}, f32[1]{0:T(128)}) all-reduce(f32[1]{0:T(128)} %bitcast.80, f32[1]{0:T(128)} %bitcast.78), channel_id=1, replica_groups=mesh['src'=8,'space'=32] {'space'}, use_global_device_ids=true, to_apply=%region_15.16 | all-reduce | flops 2 | bytes 16 | tf_op jit(solution)/shard_map/psum | solution.py:159
  231.8 0.7 fusion.106
  232.5 65.4 %all-reduce.10 = (f32[1]{0:T(128)}, f32[1]{0:T(128)}, f32[1]{0:T(128)}) all-reduce(f32[1]{0:T(128)} %bitcast.92, f32[1]{0:T(128)} %bitcast.88, f32[1]{0:T(128)} %bitcast.87), channel_id=1, replica_groups=mesh['src'=8,'space'=32] {'space'}, use_global_device_ids=true, to_apply=%region_21.22 | all-reduce | flops 3 | bytes 24 | tf_op jit(solution)/shard_map/psum | solution.py:150
  300.7 2.7 collective-permute-start.6
  303.5 3.2 collective-permute-done.6
  307.4 1.9 collective-permute-start.7
  309.3 3.1 collective-permute-done.7
  312.7 0.7 fusion.112
  313.5 61.1 %all-reduce.9 = (f32[1]{0:T(128)}, f32[1]{0:T(128)}) all-reduce(f32[1]{0:T(128)} %bitcast.114, f32[1]{0:T(128)} %bitcast.112), channel_id=1, replica_groups=mesh['src'=8,'space'=32] {'space'}, use_global_device_ids=true, to_apply=%region_25.26 | all-reduce | flops 2 | bytes 16 | tf_op jit(solution)/shard_map/psum | solution.py:159
  377.3 0.7 fusion.94
  378.0 65.4 %all-reduce.8 = (f32[1]{0:T(128)}, f32[1]{0:T(128)}, f32[1]{0:T(128)}) all-reduce(f32[1]{0:T(128)} %bitcast.121, f32[1]{0:T(128)} %bitcast.119, f32[1]{0:T(128)} %bitcast.118), channel_id=1, replica_groups=mesh['src'=8,'space'=32] {'space'}, use_global_device_ids=true, to_apply=%region_31.32 | all-reduce | flops 3 | bytes 24 | tf_op jit(solution)/shard_map/psum | solution.py:150
  446.3 2.6 collective-permute-start.8
  448.8 3.4 collective-permute-done.8
  452.9 1.9 collective-permute-start.9
  456.1 1.9 collective-permute-done.9
  458.3 0.7 fusion.100
  459.1 61.2 %all-reduce.7 = (f32[1]{0:T(128)}, f32[1]{0:T(128)}) all-reduce(f32[1]{0:T(128)} %bitcast.143, f32[1]{0:T(128)} %bitcast.141), channel_id=1, replica_groups=mesh['src'=8,'space'=32] {'space'}, use_global_device_ids=true, to_apply=%region_35.36 | all-reduce | flops 2 | bytes 16 | tf_op jit(solution)/shard_map/psum | solution.py:159
  523.0 0.7 fusion.89
  523.8 65.2 %all-reduce.6 = (f32[1]{0:T(128)}, f32[1]{0:T(128)}, f32[1]{0:T(128)}) all-reduce(f32[1]{0:T(128)} %bitcast.150, f32[1]{0:T(128)} %bitcast.148, f32[1]{0:T(128)} %bitcast.147), channel_id=1, replica_groups=mesh['src'=8,'space'=32] {'space'}, use_global_device_ids=true, to_apply=%region_41.42 | all-reduce | flops 3 | bytes 24 | tf_op jit(solution)/shard_map/psum | solution.py:150
  591.6 0.6 fusion.86
  592.3 25.7 %all-reduce.5 = f32[2,32,128]{2,1,0:T(8,128)S(1)} all-reduce(f32[2,32,128]{2,1,0:T(8,128)S(1)} %fusion.86), channel_id=2, replica_groups=mesh['src'=8,'space'=32] {'src'}, use_global_device_ids=true, to_apply=%region_43.44.clone | all-reduce | flops 8192 | bytes 65536
  618.0 0.6 constant_dynamic-slice_fusion
  (105 shorter events, 8.3 us)
Async XLA Ops:
  4.7 21.2 %all-to-all-start = ((f32[2,1,256]{0,1,2:T(1,128)}), f32[2,1,256]{0,1,2:T(1,128)S(1)}, u32[]{:S(2)}, u32[]{:S(2)}) async-start(f32[2,1,256]{0,1,2:T(1,128)} %bitcast.8), calls=%async_computation | async-start | bytes 262144 | tf_op jit(solution)/shard_map/all_to_all | solution.py:121
  14.2 6.4 %collective-permute-start = (f32[2,1,3,1,32,128]{5,4,3,0,2,1:T(8,128)S(1)}, f32[2,1,3,1,32,128]{5,4,3,0,2,1:T(8,128)S(1)}, u32[]{:S(2)}, u32[]{:S(2)}) collective-permute-start(f32[2,1,3,1,32,128]{5,4,3,0,2,1:T(8,128)S(1)} %copy.119), channel_id=1, source_target_pairs={{1,0},{2,1},{3,2},{4,3},{5,4},{6,5},{7,6},{8,7},{9,8},{10,9},{11,1... | collective-permute-start | bytes 294920 | tf_op jit(solution)/shard_map/ppermute | solution.py:12
  21.9 3.4 copy-start.3
  22.2 51.9 %collective-permute-start.1 = (f32[2,1,3,1,33,129]{5,4,3,0,2,1:T(8,128)S(1)}, f32[2,1,3,1,33,129]{5,4,3,0,2,1:T(8,128)S(1)}, u32[]{:S(2)}, u32[]{:S(2)}) collective-permute-start(f32[2,1,3,1,33,129]{5,4,3,0,2,1:T(8,128)S(1)} %slice.827), channel_id=1, source_target_pairs={{0,1},{1,2},{2,3},{3,4},{4,5},{5,6},{6,7},{7,8},{8,9},{9,10},{10,1... | collective-permute-start | bytes 306512 | tf_op jit(solution)/shard_map/ppermute | solution.py:12
  74.0 0.9 copy-start
  75.0 5.9 collective-permute-start.2
  81.7 5.0 collective-permute-start.3
  155.2 5.9 collective-permute-start.4
  161.8 5.0 collective-permute-start.5
  300.7 5.9 collective-permute-start.6
  307.4 5.0 collective-permute-start.7
  446.3 5.9 collective-permute-start.8
  452.6 2.2 copy-start.4
  452.9 5.0 collective-permute-start.9
  522.9 68.7 %copy-start.2 = (f32[2,1,3,2,32,128]{5,4,3,2,1,0:T(8,128)S(1)}, f32[2,1,3,2,32,128]{5,4,3,2,1,0:T(8,128)}, u32[]{:S(2)}) copy-start(f32[2,1,3,2,32,128]{5,4,3,2,1,0:T(8,128)} %param.9) | copy-start | bytes 589828
  591.6 27.0 %copy-start.1 = (f32[2,1,3,2,32,128]{5,4,3,2,1,0:T(8,128)}, f32[2,1,3,2,32,128]{5,4,3,2,1,0:T(8,128)S(1)}, u32[]{:S(2)}) copy-start(f32[2,1,3,2,32,128]{5,4,3,2,1,0:T(8,128)S(1)} %fusion.76) | copy-start | bytes 589828
where the time goes:
time: 624 us; the launch traced here: 619 us
  blocking collectives  470 us (75%)
  other arithmetic  55.9 us (9%)
  starting transfers between devices  31.6 us (5%)
  waiting for transfers between devices  25.1 us (4%)
  between operations  21.3 us (3%)
  local copies, waits for them, and re-layouts  15.1 us (2%)
    psum x4, blocking collectives, shards(): lax.psum((mixed_product_real, cross_im, squared(mapped)), 'space')  261 us
    psum x3, blocking collectives, shards(): turn_re, turn_im = lax.psum(inner(mapped, fresh), 'space')  183 us
    scatter-add x1, other arithmetic, shards(): jnp.zeros((2, pair_count, 3 * slab_cells), jnp.float32).at[:, :, target]  40.5 us
    unnamed x1, blocking collectives  25.7 us
    ppermute x10, waiting for transfers between devices, from_behind(): return lax.ppermute(block, axis, route)  25.1 us
    ppermute x10, starting transfers between devices, from_behind(): return lax.ppermute(block, axis, route)  23 us
  transfers between devices with their start and end apart: 11, of which 9 were waited for; matrix products, arithmetic and copies ran while one was open for 9% of the time, Pallas kernels for 0%

commit v1 on v0

v1 whole, which is shorter than its diff:
```python
import functools

import jax
import jax.numpy as jnp
from jax import lax
from jax.experimental import pallas as pl
from jax.experimental.pallas import tpu as pltpu
from jax.sharding import PartitionSpec as P

F32 = jnp.float32
SLABS = (-2, -1, 0, 1, 2, 3)
ROWS, LANES = 32, 128
BLK = (8, 128)
CAP = 8
VMEM_BYTES = 40 * 1024 * 1024


def spec(space=pltpu.VMEM):
    return pl.BlockSpec(memory_space=space)


def iota(shape, axis):
    return lax.broadcasted_iota(jnp.int32, shape, axis)


def two_sum(a, b):
    s = a + b
    t = s - a
    return s, (a - (s - t)) + (b - t)


def split(a):
    t = a * F32(4097.0)
    high = t - (t - a)
    return high, a - high


def product_error(p, a, b):
    (ah, al), (bh, bl) = a, b
    return ((ah * bh - p) + ah * bl + al * bh) + al * bl


def pair_add(a, b):
    s, e = two_sum(a[0], b[0])
    e = e + (a[1] + b[1])
    h = s + e
    return h, e - (h - s)


def pair_scale(a, c):
    p = a[0] * c
    e = product_error(p, split(a[0]), split(c)) + a[1] * c
    h = p + e
    return h, e - (h - p)


def negate(a):
    return tuple(-v for v in a)


def total(terms):
    return functools.reduce(pair_add, terms)


def mix_re(g, v):
    return pair_add(pair_scale(g[0], v[0]), negate(pair_scale(g[1], v[1])))


def mix(g, v):
    return mix_re(g, v), pair_add(pair_scale(g[0], v[1]), pair_scale(g[1], v[0]))


def csum(terms):
    return total([t[0] for t in terms]), total([t[1] for t in terms])


def conj(g):
    return g[0], negate(g[1])


def cneg(v):
    return -v[0], -v[1]


def cmul(a, b):
    return a[0] * b[0] - a[1] * b[1], a[0] * b[1] + a[1] * b[0]


def over(g, den):
    return g[0][0] / den, g[1][0] / den


def y_next(e):
    return jnp.where(iota(e.shape, 0) == ROWS - 1, F32(0), pltpu.roll(e, ROWS - 1, 0))


def z_next(e):
    return jnp.where(iota(e.shape, 1) == LANES - 1, F32(0), pltpu.roll(e, LANES - 1, 1))


def y_prev(h, first):
    return jnp.where(iota(h.shape, 0) == 0, first, pltpu.roll(h, 1, 0))


def z_prev(h, first):
    return jnp.where(iota(h.shape, 1) == 0, first, pltpu.roll(h, 1, 1))


def curl_curl(field, part, at, above, below):
    ex, ey, ez = (field[3 * part + c, at] for c in range(3))
    ey_up, ez_up = (field[3 * part + c, at + 1] * above for c in (1, 2))
    ex_dn, ey_dn, ez_dn = (field[3 * part + c, at - 1] * below for c in range(3))
    hx = (y_next(ez) - ez) - (z_next(ey) - ey)
    hy = (z_next(ex) - ex) - (ez_up - ez)
    hz = (ey_up - ey) - (y_next(ex) - ex)
    hy_dn = (z_next(ex_dn) - ex_dn) - (ez - ez_dn)
    hz_dn = (ey - ey_dn) - (y_next(ex_dn) - ex_dn)
    return (
        (hz - y_prev(hz, -ex)) - (hy - z_prev(hy, ex)),
        (hx - z_prev(hx, -ey)) - (hz - hz_dn),
        (hy - hy_dn) - (hx - y_prev(hx, ez)),
    )


def apply(me, field, damping, first, low, high, store):
    @pl.loop(low, high)
    def _(at):
        grid_plane = lax.rem(2 * me + first + at + 64, 64)
        above = jnp.where(grid_plane == 63, F32(0), F32(1))
        below = jnp.where(grid_plane == 0, F32(0), F32(1))
        damp = damping[at]
        real = curl_curl(field, 0, at, above, below)
        for c in range(3):
            store(0, c, at, real[c] - damp * field[3 + c, at])
        imag = curl_curl(field, 1, at, above, below)
        for c in range(3):
            store(1, c, at, imag[c] + damp * field[c, at])


def gram(fields, pairs, out, size=4):
    sums = []
    for first in range(0, len(pairs), size):
        group = pairs[first : first + size]
        used = sorted({k for pair in group for k in pair})
        count = sum(1 if i == j else 2 for i, j in group)

        def body(step, acc, group=group, used=used):
            comp, rest = step // 8, lax.rem(step, 8)
            plane, row = rest // 4, pl.multiple_of(lax.rem(rest, 4) * 8, 8)
            values = {}
            for k in used:
                ref, start = fields[k]
                for part in range(2):
                    v = ref[3 * part + comp, start + plane, pl.ds(row, 8), :]
                    values[k, part] = v, split(v)

            def add(acc, a, b, minus=False):
                p = a[0] * b[0]
                e = product_error(p, a[1], b[1])
                p, e = (-p, -e) if minus else (p, e)
                s, lost = two_sum(acc[0], p)
                return s, acc[1] + (lost + e)

            new = []
            for i, j in group:
                re = acc[len(new)]
                re = add(re, values[i, 0], values[j, 0])
                new.append(add(re, values[i, 1], values[j, 1]))
                if i != j:
                    im = acc[len(new)]
                    im = add(im, values[i, 0], values[j, 1])
                    new.append(add(im, values[i, 1], values[j, 0], minus=True))
            return tuple(new)

        zero = jnp.zeros(BLK, F32)
        sums += list(lax.fori_loop(0, 24, body, tuple((zero, zero) for _ in range(count))))
    packed = []
    for first in range(0, len(sums), 8):
        high = low = jnp.zeros(BLK, F32)
        for k, s in enumerate(sums[first : first + 8]):
            for shift in (4, 2, 1):
                s = pair_add(s, tuple(pltpu.roll(v, shift, 0) for v in s))
            here = iota(BLK, 0) == k
            high, low = jnp.where(here, s[0], high), jnp.where(here, s[1], low)
        packed.append((high, low))
    line = jnp.zeros(BLK, F32)
    for n, s in enumerate(packed):
        for shift in (64, 32, 16, 8, 4, 2, 1):
            s = pair_add(s, tuple(pltpu.roll(v, shift, 1) for v in s))
        away = iota(BLK, 1) - iota(BLK, 0) - 8 * n
        line = line + jnp.where(away == 0, s[0], F32(0)) + jnp.where(away == 64, s[1], F32(0))
    line = jnp.sum(line, axis=0, keepdims=True)
    out[...] = jnp.broadcast_to(line, out.shape)


def gathered(parts, pairs):
    lines = []
    for n in range(parts.shape[0] // 8):
        high = parts[8 * n : 8 * n + 8, :]
        lines.append((high, pltpu.roll(high, 64, 1)))
    s = total(lines)
    for shift in (4, 2, 1):
        s = pair_add(s, tuple(pltpu.roll(v, shift, 0) for v in s))
    entries, at = {}, 0

    def lane(k):
        return tuple(jnp.broadcast_to(v[:, k : k + 1], BLK) for v in s)

    zero = (jnp.zeros(BLK, F32), jnp.zeros(BLK, F32))
    for i, j in pairs:
        re, at = lane(at), at + 1
        im = zero
        if i != j:
            im, at = lane(at), at + 1
        entries[i, j] = (re, im)
        entries[j, i] = (re, negate(im)) if i != j else (re, im)
    return entries


def rows(v):
    return tuple(jnp.concatenate([x] * (ROWS // 8), axis=0) for x in v)


def scaled(v, re, im):
    return v[0] * re - v[1] * im, v[0] * im + v[1] * re


PAIRS_1 = ((1, 1), (2, 2), (0, 1), (1, 2), (0, 2))
PAIRS_2 = ((1, 1), (2, 2), (3, 3), (4, 4), (0, 1), (0, 2), (1, 2), (0, 3), (0, 4), (1, 3), (1, 4), (2, 3), (2, 4), (3, 4))


def scatter_source(me, n_slabs, weights, slab_of, cell_of, comp_of, source):
    upper = (iota((LANES, LANES), 0) <= iota((LANES, LANES), 1)).astype(jnp.bfloat16)
    key = (comp_of[...] * 8192 + cell_of[...]).astype(F32)
    n_blocks = key.shape[0]
    slots = n_blocks * CAP

    @pl.loop(0, len(SLABS))
    def _(s):
        slab = lax.rem(me + s + SLABS[0] + n_slabs, n_slabs)
        mine = slab_of[...] == slab
        mine_f = jnp.where(mine, F32(1), F32(0))
        rank = jnp.dot(mine_f.astype(jnp.bfloat16), upper, preferred_element_type=F32)
        rank = jnp.where(mine, rank, F32(0))
        slot = (iota((n_blocks, CAP, LANES), 1) + 1).astype(F32)
        chosen = rank[:, None, :] == slot

        def column(values):
            v = jnp.where(chosen, values[:, None, :], F32(0))
            return jnp.sum(v, axis=2, keepdims=True).reshape(slots, 1)

        place = column(key).astype(jnp.int32)
        hot_z = (place & (LANES - 1)) == iota((slots, LANES), 1)
        hot_row = jnp.where((place >> 7) == iota((slots, 256), 1), F32(1), F32(0))
        put = jnp.concatenate(
            [jnp.where(hot_z, column(weights[:, part, :]), F32(0)) for part in range(2)], axis=1
        )
        grid = lax.dot_general(
            hot_row,
            put,
            (((0,), (0,)), ((), ())),
            precision=lax.Precision.HIGHEST,
            preferred_element_type=F32,
        )
        for part in range(2):
            for comp in range(3):
                for plane in range(2):
                    row = comp * 64 + plane * 32
                    source[3 * part + comp, 2 * s + plane] = grid[
                        row : row + 32, part * LANES : (part + 1) * LANES
                    ]


def start_kernel(
    n_slabs, own, b2, b1, a1, a2, a3, weights, slab_of, cell_of, comp_of, freqs, pair,
    p0_out, p1_out, p2_out, damp_out, gram_out,
    field, damping, source, p0, p1,
):
    me = lax.axis_index("space")
    wave = freqs[pair[0]]
    for s, ref in enumerate((b2, b1, own, a1, a2, a3)):
        for k in range(6):
            field[k, 2 * s : 2 * s + 2] = ref[2 * k : 2 * k + 2]
        damping[2 * s : 2 * s + 2] = ref[12:14] * wave
    scatter_source(me, n_slabs, weights, slab_of, cell_of, comp_of, source)

    def keep_p0(part, comp, at, value):
        p0[3 * part + comp, at] = source[3 * part + comp, at] - value

    def keep_p1(part, comp, at, value):
        p1[3 * part + comp, at] = value

    def keep_p2(part, comp, at, value):
        p2_out[3 * part + comp, at - 3] = value

    apply(me, field, damping, -4, 1, 11, keep_p0)
    apply(me, p0, damping, -4, 2, 10, keep_p1)
    apply(me, p1, damping, -4, 3, 9, keep_p2)
    for k in range(6):
        p0_out[k] = p0[k, 3:9]
        p1_out[k] = p1[k, 3:9]
    damp_out[...] = damping[3:9]
    gram(((p0, 5), (p1, 5), (p2_out, 2)), PAIRS_1, gram_out)


def middle_kernel(
    parts, p0, p1, p2, damping, own,
    xs_out, r_out, d_out, m_out, f_out, gram_out,
    r, m, f, g, h,
):
    me = lax.axis_index("space")
    e = gathered(parts, PAIRS_1)
    den = e[1, 1][0][0]
    a = over(e[1, 0], den)
    t = csum([e[1, 1], mix(e[1, 2], cneg(a))])
    b = cneg(over(t, den))
    u = (F32(1) + b[0], b[1])
    w = [conj(csum([mix(e[i, 1], u), mix(e[i, 2], cneg(a))])) for i in range(3)]
    num = csum([w[0], mix(w[1], cneg(a))])
    den = pair_add(mix_re(w[1], u), mix_re(w[2], cneg(a)))[0]
    step = over(num, den)
    su = cmul(step, u)
    s = (a[0] + su[0], a[1] + su[1])
    v = cmul(step, a)
    a, u, s, v = rows(a), rows(u), rows(s), rows(v)

    @pl.loop(0, 6)
    def _(at):
        for c in range(3):
            v0 = (p0[c, at], p0[3 + c, at])
            v1 = (p1[c, at], p1[3 + c, at])
            v2 = (p2[c, at], p2[3 + c, at])
            s1, w2 = scaled(s, *v1), scaled(v, *v2)
            u1, a2 = scaled(u, *v1), scaled(a, *v2)
            for part in range(2):
                r[3 * part + c, at] = (v0[part] - s1[part]) + w2[part]
                m[3 * part + c, at] = u1[part] - a2[part]

    for plane in range(2):
        for c in range(3):
            v0 = (p0[c, 1 + plane], p0[3 + c, 1 + plane])
            v1 = (p1[c, 1 + plane], p1[3 + c, 1 + plane])
            s0, w1 = scaled(s, *v0), scaled(v, *v1)
            u0, a1 = scaled(u, *v0), scaled(a, *v1)
            for part in range(2):
                k = 2 * (3 * part + c) + plane
                xs_out[k] = (own[k] + s0[part]) - w1[part]
                d_out[k] = u0[part] - a1[part]
                r_out[k] = r[3 * part + c, 1 + plane]
                m_out[k] = m[3 * part + c, 1 + plane]

    def into(ref):
        def store(part, comp, at, value):
            ref[3 * part + comp, at] = value

        return store

    apply(me, r, damping, -1, 1, 5, into(f))
    apply(me, m, damping, -1, 2, 4, into(g))
    apply(me, f, damping, -1, 2, 4, into(h))
    for k in range(6):
        f_out[2 * k : 2 * k + 2] = f[k, 1:3]
    gram(((r, 2), (m, 2), (f, 2), (g, 2), (h, 2)), PAIRS_2, gram_out)


def end_kernel(parts, xs, r, d, m, f, background, freqs, pair, adjoint_out, terms_out):
    wave = freqs[pair[0]]
    e = gathered(parts, PAIRS_2)
    b = cneg(over(e[1, 2], e[1, 1][0][0]))
    w = [conj(csum([mix(e[i, 1], b), e[i, 2]])) for i in range(5)]
    den = pair_add(mix_re(w[1], b), w[2][0])[0]
    a = over(w[0], den)
    ab = cmul(a, b)
    t = csum([w[2], mix(w[3], cneg(ab)), mix(w[4], cneg(a))])
    b2 = cneg(over(t, den))
    q1, q2 = (F32(1) + b2[0], b2[1]), cmul(b2, b)
    mapped = (q2, q1, cneg(ab), cneg(a))
    w = [conj(csum([mix(e[i, 1 + k], q) for k, q in enumerate(mapped)])) for i in range(5)]
    num = csum([w[0], mix(w[1], cneg(ab)), mix(w[2], cneg(a))])
    den = total([mix_re(w[1 + k], q) for k, q in enumerate(mapped)])[0]
    a2 = over(num, den)
    to_r, to_d = cmul(a2, q1), cmul(a2, q2)
    to_r = rows((a[0] + to_r[0], a[1] + to_r[1]))
    to_d = rows((ab[0] + to_d[0], ab[1] + to_d[1]))
    to_f, to_m = rows(cmul(a2, a)), rows(cmul(a2, ab))
    for plane in range(2):
        terms = jnp.zeros((ROWS, LANES), F32)
        for c in range(3):
            k, q = 2 * c + plane, 2 * (3 + c) + plane
            add = [
                scaled(to_r, r[k], r[q]),
                scaled(to_d, d[k], d[q]),
                cneg(scaled(to_f, f[k], f[q])),
                cneg(scaled(to_m, m[k], m[q])),
            ]
            re = xs[k] + ((add[0][0] + add[1][0]) + (add[2][0] + add[3][0]))
            im = xs[q] + ((add[0][1] + add[1][1]) + (add[2][1] + add[3][1]))
            adjoint_out[k] = re
            adjoint_out[q] = im
            terms = terms + (re * background[q] + im * background[k])
        terms = terms * wave
        n_src = terms_out.shape[0]
        part = ROWS // n_src
        for n in range(n_src):
            terms_out[n, plane * part : (plane + 1) * part] = terms[n * part : (n + 1) * part]


def shaped(*shape):
    return jax.ShapeDtypeStruct(shape, F32)


def kernel(body, name, in_specs, outs, scratch, flops):
    return pl.pallas_call(
        body,
        name=name,
        in_specs=in_specs,
        out_specs=tuple(spec() for _ in outs),
        out_shape=tuple(outs),
        scratch_shapes=[pltpu.VMEM(s, F32) for s in scratch],
        compiler_params=pltpu.CompilerParams(vmem_limit_bytes=VMEM_BYTES),
        cost_estimate=pl.CostEstimate(flops=flops, bytes_accessed=3_000_000, transcendentals=0),
    )


def shards(
    background,
    warm_start,
    conductivity,
    frequencies,
    pair_freq,
    weighted_residual,
    datum_layer_index,
    receiver_flat_cell,
    receiver_component,
):
    n_slabs, n_src = lax.axis_size("space"), lax.axis_size("src")
    own = warm_start.reshape(12, ROWS, LANES)
    message = jnp.concatenate([own, conductivity], axis=0)

    def from_slab(away):
        route = [((i + away) % n_slabs, i) for i in range(n_slabs)]
        return lax.ppermute(message, "space", route)

    window = [from_slab(away) for away in (-2, -1, 1, 2, 3)]
    weights = jnp.broadcast_to(weighted_residual.reshape(1, 2, LANES), (n_slabs, 2, LANES))
    weights = lax.all_to_all(weights, "space", split_axis=0, concat_axis=0, tiled=True)
    plane = (ROWS, LANES)
    slab_of = datum_layer_index.reshape(n_slabs, LANES)
    cell_of = receiver_flat_cell.reshape(n_slabs, LANES)
    comp_of = receiver_component.reshape(n_slabs, LANES)
    smem = spec(pltpu.SMEM)
    six = shaped(6, 6, *plane)
    p0, p1, p2, damping, parts = kernel(
        functools.partial(start_kernel, n_slabs),
        "start",
        [spec()] * 10 + [smem] * 2,
        [six, six, six, shaped(6, *plane), shaped(n_slabs, LANES)],
        [(6, 12, *plane), (12, *plane), (6, 12, *plane), (6, 12, *plane), (6, 12, *plane)],
        60_000_000,
    )(message, *window, weights, slab_of, cell_of, comp_of, frequencies, pair_freq)
    parts = lax.all_to_all(parts, "space", split_axis=0, concat_axis=0, tiled=True)
    two = shaped(12, *plane)
    xs, r, d, m, f, parts = kernel(
        middle_kernel,
        "middle",
        [spec()] * 6,
        [two] * 5 + [shaped(n_slabs, LANES)],
        [(6, 6, *plane)] * 5,
        40_000_000,
    )(parts, p0, p1, p2, damping, own)
    parts = lax.all_to_all(parts, "space", split_axis=0, concat_axis=0, tiled=True)
    adjoint, terms = kernel(
        end_kernel,
        "end",
        [spec()] * 7 + [smem] * 2,
        [two, shaped(n_src, 2 * (ROWS // n_src), LANES)],
        [],
        5_000_000,
    )(parts, xs, r, d, m, f, background.reshape(12, *plane), frequencies, pair_freq)
    terms = lax.all_to_all(terms, "src", split_axis=0, concat_axis=0, tiled=True)
    gradient = jnp.sum(terms, axis=0).reshape(2, ROWS // n_src, LANES)
    return adjoint.reshape(warm_start.shape), gradient


def solution(mesh):
    placed = (
        P(None, "src", None, "space", None, None),
        P(None, "src", None, "space", None, None),
        P("space", None, None),
        P(),
        P("src"),
        P(None, "src", "space"),
        P(),
        P(),
        P(),
    )
    return jax.shard_map(
        shards,
        mesh=mesh,
        in_specs=placed,
        out_specs=(P(None, "src", None, "space", None, None), P("space", "src", None)),
        check_vma=False,
    )
```

time: 624 us -> 84.2 us (0.13)
  blocking collectives: 470 us -> 36.5 us
  other arithmetic: 55.9 us -> 1.57 us
  Pallas kernels: 0 us -> 21.2 us
  between operations: 21.3 us -> 1.36 us
  waiting for transfers between devices: 25.1 us -> 6.64 us
  starting transfers between devices: 31.6 us -> 15.3 us
  local copies, waits for them, and re-layouts: 15.1 us -> 1.27 us
    psum x7 -> x0, blocking collectives: 444 us -> none  [the longest x4 261 us: shards(): lax.psum((mixed_product_real, cross_im, squared(mapped)), 'space')]
    scatter-add x1 -> x0, other arithmetic: 40.5 us -> none  [shards(): jnp.zeros((2, pair_count, 3 * slab_cells), jnp.float32).at[:, :, target]]
    all_to_all x0 -> x3, blocking collectives: none -> 36.5 us  [the longest x2 21.6 us: shards(): lax.all_to_all(parts, 'space', split_axis=0, concat_axis=0, tiled=True)]
    unnamed x1 -> x0, blocking collectives: 25.7 us -> none
    ppermute x10 -> x5, waiting for transfers between devices: 25.1 us -> 0.01 us  [from_slab(): return lax.ppermute(message, 'space', route)]
    pallas_call x0 -> x3, Pallas kernels: none -> 21.2 us  [the longest x1 11.4 us: shards(): kernel(functools.partial(start_kernel, n_slabs), 'start', [spec()] * 10 +...]
    ppermute x10 -> x5, starting transfers between devices: 23 us -> 9.61 us  [from_slab(): return lax.ppermute(message, 'space', route)]
    reshape x1 -> x0, local copies, waits for them, and re-layouts: 7.59 us -> none  [shards(): source = flat_src.reshape(2, pair_count, 3, planes, rows_y, rows_z)]
  transfers between devices with their start and end apart: 11 -> 6, of which waited for: 9 -> 1; matrix products, arithmetic and copies ran while one was open for 9% -> 1% of each run, Pallas kernels for 0% -> 0%
where the time goes in v1:
time: 84.2 us; the launch traced here: 83.8 us
  blocking collectives  36.5 us (43%)
  Pallas kernels  21.2 us (25%)
  starting transfers between devices  15.3 us (18%)
  waiting for transfers between devices  6.64 us (8%)
  other arithmetic  1.57 us (2%)
  between operations  1.36 us (2%)
  local copies, waits for them, and re-layouts  1.27 us (2%)
    all_to_all x2, blocking collectives, shards(): lax.all_to_all(parts, 'space', split_axis=0, concat_axis=0, tiled=True)  21.6 us
    all_to_all x1, blocking collectives, shards(): lax.all_to_all(terms, 'src', split_axis=0, concat_axis=0, tiled=True)  14.9 us
    pallas_call x1, Pallas kernels, shards(): kernel(functools.partial(start_kernel, n_slabs), 'start', [spec()] * 10 +...  11.4 us
    ppermute x5, starting transfers between devices, from_slab(): return lax.ppermute(message, 'space', route)  9.61 us
    pallas_call x1, Pallas kernels, shards(): kernel(middle_kernel, 'middle', [spec()] * 6, [two] * 5 + [shaped(n_slabs...  7.8 us
    all_to_all x1, waiting for transfers between devices, shards(): lax.all_to_all(weights, 'space', split_axis=0, concat_axis=0, tiled=True)  6.63 us
    all_to_all x1, starting transfers between devices, shards(): lax.all_to_all(weights, 'space', split_axis=0, concat_axis=0, tiled=True)  5.74 us
    pallas_call x1, Pallas kernels, shards(): kernel(end_kernel, 'end', [spec()] * 7 + [smem] * 2, [two, shaped(n_src,...  2 us
  transfers between devices with their start and end apart: 6, of which 1 were waited for; matrix products, arithmetic and copies ran while one was open for 1% of the time, Pallas kernels for 0%

profile of v1, /device:TPU:1, one launch (start us, length us, event | category | flops | bytes accessed | tf_op | source)
XLA Modules:
  0.0 83.8 jit_solution(9471963359024561959)
XLA Ops:
  0.6 1.0 %pad_maximum_fusion.own = f32[14,32,128]{2,1,0:T(8,128)S(1)} fusion(f32[2,32,128]{2,1,0:T(8,128)} %param.11, f32[12,32,128]{2,1,0:T(8,128)} %bitcast.18), kind=kLoop, calls=%fused_computation | loop fusion | flops 57344 | bytes 458752 | tf_op jit(solution)/shard_map/concatenate | solution.py:438
  1.6 0.0 copy-start.6
  1.6 6.4 %collective-permute-start.4 = (f32[14,32,128]{2,1,0:T(8,128)S(1)}, f32[14,32,128]{2,1,0:T(8,128)S(1)}, u32[]{:S(2)}, u32[]{:S(2)}) collective-permute-start(f32[14,32,128]{2,1,0:T(8,128)S(1)} %pad_maximum_fusion.own), channel_id=1, source_target_pairs={{3,0},{4,1},{5,2},{6,3},{7,4},{8,5},{9,6},{10,7},{11,8},{12,9},{13... | collective-permute-start | bytes 688136 | tf_op jit(solution)/shard_map/ppermute | solution.py:442
  8.0 0.5 collective-permute-start.3
  8.5 0.6 collective-permute-start.2
  9.1 1.1 %collective-permute-start.1 = (f32[14,32,128]{2,1,0:T(8,128)S(1)}, f32[14,32,128]{2,1,0:T(8,128)S(1)}, u32[]{:S(2)}, u32[]{:S(2)}) collective-permute-start(f32[14,32,128]{2,1,0:T(8,128)S(1)} %pad_maximum_fusion.own), channel_id=1, source_target_pairs={{31,0},{0,1},{1,2},{2,3},{3,4},{4,5},{5,6},{6,7},{7,8},{8,9},{9,10... | collective-permute-start | bytes 688136 | tf_op jit(solution)/shard_map/ppermute | solution.py:442
  10.2 1.0 %collective-permute-start = (f32[14,32,128]{2,1,0:T(8,128)S(1)}, f32[14,32,128]{2,1,0:T(8,128)S(1)}, u32[]{:S(2)}, u32[]{:S(2)}) collective-permute-start(f32[14,32,128]{2,1,0:T(8,128)S(1)} %pad_maximum_fusion.own), channel_id=1, source_target_pairs={{30,0},{31,1},{0,2},{1,3},{2,4},{3,5},{4,6},{5,7},{6,8},{7,9},{8,1... | collective-permute-start | bytes 688136 | tf_op jit(solution)/shard_map/ppermute | solution.py:442
  11.2 0.0 copy-done.6
  11.2 0.6 broadcast_in_dim.8
  11.8 0.0 copy-start.2
  11.8 0.0 copy-start.3
  11.8 0.0 copy-start.4
  11.9 5.7 %all-to-all-start = ((f32[32,2,128]{2,1,0:T(2,128)}), f32[32,2,128]{2,1,0:T(2,128)S(1)}, u32[]{:S(2)}, u32[]{:S(2)}) async-start(f32[32,2,128]{2,1,0:T(2,128)} %broadcast_in_dim.8), calls=%async_computation | async-start | bytes 65536 | tf_op jit(solution)/shard_map/all_to_all | solution.py:446
  18.2 6.6 %all-to-all-done.weights = f32[32,2,128]{2,1,0:T(2,128)S(1)} async-done(((f32[32,2,128]{2,1,0:T(2,128)}), f32[32,2,128]{2,1,0:T(2,128)S(1)}, u32[]{:S(2)}, u32[]{:S(2)}) %all-to-all-start) | async-done | bytes 32800 | tf_op jit(solution)/shard_map/all_to_all | solution.py:446
  24.9 0.0 collective-permute-done.4.a3
  24.9 0.0 collective-permute-done.3.a2
  24.9 0.0 collective-permute-done.2.a1
  24.9 0.0 collective-permute-done.1.b1
  24.9 0.0 collective-permute-done.b2
  24.9 0.0 copy-start.5
  24.9 0.0 copy-done.2
  24.9 0.0 copy-done.3
  24.9 0.0 copy-done.4
  24.9 0.6 copy-done.5
  25.6 0.0 copy-start
  25.6 11.4 %start.1 = (f32[6,6,32,128]{3,2,1,0:T(8,128)S(1)}, f32[6,6,32,128]{3,2,1,0:T(8,128)S(1)}, f32[6,6,32,128]{3,2,1,0:T(8,128)S(1)}, f32[6,32,128]{2,1,0:T(8,128)S(1)}, f32[32,128]{1,0:T(8,128)S(1)}) custom-call(f32[14,32,128]{2,1,0:T(8,128)S(1)} %pad_maximum_fusion.own, f32[14,32,128]{2,1,0:T(8,128)S(1)} %collective-permute-done.b2, ...), custom_call_target="tpu_custom_call" | custom-call | flops 60000000 | bytes 3000000 | tf_op jit(solution)/shard_map/start/pallas_call | solution.py:453
  36.9 10.9 %all_to_all.32 = f32[32,1,128]{2,1,0:T(1,128)S(1)} all-to-all(f32[32,1,128]{2,1,0:T(1,128)S(1)} %bitcast.26), channel_id=1, replica_groups=mesh['src'=8,'space'=32] {'space'}, dimensions={0} | all-to-all | bytes 32768 | tf_op jit(solution)/shard_map/all_to_all | solution.py:461
  47.9 0.0 copy-done
  47.9 0.0 copy-start.1
  47.9 7.8 %middle.1 = (f32[12,32,128]{2,1,0:T(8,128)S(1)}, f32[12,32,128]{2,1,0:T(8,128)S(1)}, f32[12,32,128]{2,1,0:T(8,128)S(1)}, f32[12,32,128]{2,1,0:T(8,128)S(1)}, f32...) custom-call(f32[32,128]{1,0:T(8,128)S(1)} %bitcast.21, f32[6,6,32,128]{3,2,1,0:T(8,128)S(1)} %get-tuple-element.16.p0, ...), custom_call_target="tpu_custom_call" | custom-call | flops 40000000 | bytes 3000000 | tf_op jit(solution)/shard_map/middle/pallas_call | solution.py:463
  55.7 10.7 %all_to_all.33 = f32[32,1,128]{2,1,0:T(1,128)S(1)} all-to-all(f32[32,1,128]{2,1,0:T(1,128)S(1)} %bitcast.27), channel_id=1, replica_groups=mesh['src'=8,'space'=32] {'space'}, dimensions={0} | all-to-all | bytes 32768 | tf_op jit(solution)/shard_map/all_to_all | solution.py:471
  66.4 0.0 copy-done.1
  66.4 2.0 %end.1 = (f32[12,32,128]{2,1,0:T(8,128)}, f32[8,8,128]{2,1,0:T(8,128)S(1)}) custom-call(f32[32,128]{1,0:T(8,128)S(1)} %bitcast.22, f32[12,32,128]{2,1,0:T(8,128)S(1)} %get-tuple-element.21.xs, f32[12,32,128]{2,1,0:T(8,128)S(1)} %get-tuple-element.22.r, f32[12,32,128]{2,1,0:T(8,128)S(1)} %get-tuple-element.23.d, f32[12,32,128]{2,1,0:T(8,128)S(1)} %get-tuple-element.24.m, ...), custom_call_target="tpu_custom_call" | custom-call | flops 5000000 | bytes 3000000 | tf_op jit(solution)/shard_map/end/pallas_call | solution.py:472
  68.4 14.9 %all_to_all.34 = f32[8,8,128]{2,1,0:T(8,128)S(1)} all-to-all(f32[8,8,128]{2,1,0:T(8,128)S(1)} %get-tuple-element.27), channel_id=1, replica_groups=mesh['src'=8,'space'=32] {'src'}, dimensions={0} | all-to-all | bytes 65536 | tf_op jit(solution)/shard_map/all_to_all | solution.py:480
  83.2 0.6 reduce_sum.9
Async XLA Ops:
  1.6 9.6 %copy-start.6 = (f32[2,1,128]{2,1,0:T(1,128)S(1)}, f32[2,1,128]{2,1,0:T(1,128)}, u32[]{:S(2)}) copy-start(f32[2,1,128]{2,1,0:T(1,128)} %param.14) | copy-start | bytes 3076
  1.6 23.3 %collective-permute-start.4 = (f32[14,32,128]{2,1,0:T(8,128)S(1)}, f32[14,32,128]{2,1,0:T(8,128)S(1)}, u32[]{:S(2)}, u32[]{:S(2)}) collective-permute-start(f32[14,32,128]{2,1,0:T(8,128)S(1)} %pad_maximum_fusion.own), channel_id=1, source_target_pairs={{3,0},{4,1},{5,2},{6,3},{7,4},{8,5},{9,6},{10,7},{11,8},{12,9},{13... | collective-permute-start | bytes 688136 | tf_op jit(solution)/shard_map/ppermute | solution.py:442
  8.0 16.9 %collective-permute-start.3 = (f32[14,32,128]{2,1,0:T(8,128)S(1)}, f32[14,32,128]{2,1,0:T(8,128)S(1)}, u32[]{:S(2)}, u32[]{:S(2)}) collective-permute-start(f32[14,32,128]{2,1,0:T(8,128)S(1)} %pad_maximum_fusion.own), channel_id=1, source_target_pairs={{2,0},{3,1},{4,2},{5,3},{6,4},{7,5},{8,6},{9,7},{10,8},{11,9},{12,... | collective-permute-start | bytes 688136 | tf_op jit(solution)/shard_map/ppermute | solution.py:442
  8.5 16.4 %collective-permute-start.2 = (f32[14,32,128]{2,1,0:T(8,128)S(1)}, f32[14,32,128]{2,1,0:T(8,128)S(1)}, u32[]{:S(2)}, u32[]{:S(2)}) collective-permute-start(f32[14,32,128]{2,1,0:T(8,128)S(1)} %pad_maximum_fusion.own), channel_id=1, source_target_pairs={{1,0},{2,1},{3,2},{4,3},{5,4},{6,5},{7,6},{8,7},{9,8},{10,9},{11,1... | collective-permute-start | bytes 688136 | tf_op jit(solution)/shard_map/ppermute | solution.py:442
  9.1 15.8 %collective-permute-start.1 = (f32[14,32,128]{2,1,0:T(8,128)S(1)}, f32[14,32,128]{2,1,0:T(8,128)S(1)}, u32[]{:S(2)}, u32[]{:S(2)}) collective-permute-start(f32[14,32,128]{2,1,0:T(8,128)S(1)} %pad_maximum_fusion.own), channel_id=1, source_target_pairs={{31,0},{0,1},{1,2},{2,3},{3,4},{4,5},{5,6},{6,7},{7,8},{8,9},{9,10... | collective-permute-start | bytes 688136 | tf_op jit(solution)/shard_map/ppermute | solution.py:442
  10.2 14.7 %collective-permute-start = (f32[14,32,128]{2,1,0:T(8,128)S(1)}, f32[14,32,128]{2,1,0:T(8,128)S(1)}, u32[]{:S(2)}, u32[]{:S(2)}) collective-permute-start(f32[14,32,128]{2,1,0:T(8,128)S(1)} %pad_maximum_fusion.own), channel_id=1, source_target_pairs={{30,0},{31,1},{0,2},{1,3},{2,4},{3,5},{4,6},{5,7},{6,8},{7,9},{8,1... | collective-permute-start | bytes 688136 | tf_op jit(solution)/shard_map/ppermute | solution.py:442
  11.8 13.1 %copy-start.2 = (s32[4096,1]{0,1:T(1,128)S(1)}, s32[4096,1]{0,1:T(1,128)}, u32[]{:S(2)}) copy-start(s32[4096,1]{0,1:T(1,128)} %param.15) | copy-start | bytes 49156
  11.8 13.1 %copy-start.3 = (s32[4096]{0:T(1024)S(1)}, s32[4096]{0:T(1024)}, u32[]{:S(2)}) copy-start(s32[4096]{0:T(1024)} %param.16) | copy-start | bytes 49156
  11.8 13.1 %copy-start.4 = (s32[4096]{0:T(1024)S(1)}, s32[4096]{0:T(1024)}, u32[]{:S(2)}) copy-start(s32[4096]{0:T(1024)} %param.17) | copy-start | bytes 49156
  11.9 13.0 %all-to-all-start = ((f32[32,2,128]{2,1,0:T(2,128)}), f32[32,2,128]{2,1,0:T(2,128)S(1)}, u32[]{:S(2)}, u32[]{:S(2)}) async-start(f32[32,2,128]{2,1,0:T(2,128)} %broadcast_in_dim.8), calls=%async_computation | async-start | bytes 65536 | tf_op jit(solution)/shard_map/all_to_all | solution.py:446
  24.9 0.7 copy-start.5
  25.6 22.3 %copy-start = (f32[2,1,3,2,32,128]{5,4,3,2,1,0:T(8,128)S(1)}, f32[2,1,3,2,32,128]{5,4,3,2,1,0:T(8,128)}, u32[]{:S(2)}) copy-start(f32[2,1,3,2,32,128]{5,4,3,2,1,0:T(8,128)} %param.10) | copy-start | bytes 589828
  47.9 18.5 %copy-start.1 = (f32[2,1,3,2,32,128]{5,4,3,2,1,0:T(8,128)S(1)}, f32[2,1,3,2,32,128]{5,4,3,2,1,0:T(8,128)}, u32[]{:S(2)}) copy-start(f32[2,1,3,2,32,128]{5,4,3,2,1,0:T(8,128)} %param.9) | copy-start | bytes 589828

commit v2 on v1

--- a/solution.py
+++ b/solution.py
@@ -12,7 +12,7 @@
 ROWS, LANES = 32, 128
 BLK = (8, 128)
 CAP = 8
-VMEM_BYTES = 40 * 1024 * 1024
+VMEM_BYTES = 14 * 1024 * 1024
 
 
 def spec(space=pltpu.VMEM):
@@ -106,38 +106,67 @@
     return jnp.where(iota(h.shape, 1) == 0, first, pltpu.roll(h, 1, 1))
 
 
-def curl_curl(field, part, at, above, below):
+def forward_yz(ex, ey, ez, ey_up, ez_up):
+    hy = (z_next(ex) - ex) - (ez_up - ez)
+    hz = (ey_up - ey) - (y_next(ex) - ex)
+    return hy, hz
+
+
+def curl_curl(field, part, at, above, below, before):
     ex, ey, ez = (field[3 * part + c, at] for c in range(3))
     ey_up, ez_up = (field[3 * part + c, at + 1] * above for c in (1, 2))
-    ex_dn, ey_dn, ez_dn = (field[3 * part + c, at - 1] * below for c in range(3))
     hx = (y_next(ez) - ez) - (z_next(ey) - ey)
-    hy = (z_next(ex) - ex) - (ez_up - ez)
-    hz = (ey_up - ey) - (y_next(ex) - ex)
-    hy_dn = (z_next(ex_dn) - ex_dn) - (ez - ez_dn)
-    hz_dn = (ey - ey_dn) - (y_next(ex_dn) - ex_dn)
-    return (
+    hy, hz = forward_yz(ex, ey, ez, ey_up, ez_up)
+    edge = F32(1) - below
+    hy_dn = before[0] * below - ez * edge
+    hz_dn = before[1] * below + ey * edge
+    result = (
         (hz - y_prev(hz, -ex)) - (hy - z_prev(hy, ex)),
         (hx - z_prev(hx, -ey)) - (hz - hz_dn),
         (hy - hy_dn) - (hx - y_prev(hx, ez)),
     )
+    return result, (hy, hz)
 
 
 def apply(me, field, damping, first, low, high, store):
-    @pl.loop(low, high)
-    def _(at):
+    def plane(at, before):
         grid_plane = lax.rem(2 * me + first + at + 64, 64)
         above = jnp.where(grid_plane == 63, F32(0), F32(1))
         below = jnp.where(grid_plane == 0, F32(0), F32(1))
         damp = damping[at]
-        real = curl_curl(field, 0, at, above, below)
+        real, real_h = curl_curl(field, 0, at, above, below, before[:2])
         for c in range(3):
             store(0, c, at, real[c] - damp * field[3 + c, at])
-        imag = curl_curl(field, 1, at, above, below)
+        imag, imag_h = curl_curl(field, 1, at, above, below, before[2:])
         for c in range(3):
             store(1, c, at, imag[c] + damp * field[c, at])
+        return real_h + imag_h
+
+    below_first = []
+    for part in range(2):
+        under = [field[3 * part + c, low - 1] for c in range(3)]
+        below_first += forward_yz(*under, *(field[3 * part + c, low] for c in (1, 2)))
+    lax.fori_loop(low, high, plane, tuple(below_first))
 
 
 def gram(fields, pairs, out, size=4):
+    names = sorted({k for pair in pairs for k in pair})
+
+    def block(step, k, part):
+        comp, rest = step // 8, lax.rem(step, 8)
+        plane, row = rest // 4, pl.multiple_of(lax.rem(rest, 4) * 8, 8)
+        ref, start = fields[k]
+        return ref[3 * part + comp, start + plane, pl.ds(row, 8), :]
+
+    def peak(step, tops):
+        return tuple(
+            jnp.maximum(top, jnp.maximum(jnp.abs(block(step, k, 0)), jnp.abs(block(step, k, 1))))
+            for k, top in zip(names, tops)
+        )
+
+    zero = jnp.zeros(BLK, F32)
+    tops = lax.fori_loop(0, 24, peak, tuple(zero for _ in names), unroll=2)
+    grids = {k: top * F32(2.0**15) for k, top in zip(names, tops)}
     sums = []
     for first in range(0, len(pairs), size):
         group = pairs[first : first + size]
@@ -145,35 +174,30 @@
         count = sum(1 if i == j else 2 for i, j in group)
 
         def body(step, acc, group=group, used=used):
-            comp, rest = step // 8, lax.rem(step, 8)
-            plane, row = rest // 4, pl.multiple_of(lax.rem(rest, 4) * 8, 8)
             values = {}
             for k in used:
-                ref, start = fields[k]
                 for part in range(2):
-                    v = ref[3 * part + comp, start + plane, pl.ds(row, 8), :]
-                    values[k, part] = v, split(v)
-
-            def add(acc, a, b, minus=False):
-                p = a[0] * b[0]
-                e = product_error(p, a[1], b[1])
-                p, e = (-p, -e) if minus else (p, e)
-                s, lost = two_sum(acc[0], p)
-                return s, acc[1] + (lost + e)
+                    v = block(step, k, part)
+                    high = (v + grids[k]) - grids[k]
+                    values[k, part] = v, high, v - high
+
+            def products(a, b):
+                return a[1] * b[1], a[1] * b[2] + a[2] * b[0]
 
             new = []
             for i, j in group:
+                x, y = products(values[i, 0], values[j, 0]), products(values[i, 1], values[j, 1])
                 re = acc[len(new)]
-                re = add(re, values[i, 0], values[j, 0])
-                new.append(add(re, values[i, 1], values[j, 1]))
+                new.append(tuple(re[n] + (x[n] + y[n]) for n in range(2)))
                 if i != j:
+                    x, y = products(values[i, 0], values[j, 1]), products(values[i, 1], values[j, 0])
                     im = acc[len(new)]
-                    im = add(im, values[i, 0], values[j, 1])
-                    new.append(add(im, values[i, 1], values[j, 0], minus=True))
+                    new.append(tuple(im[n] + (x[n] - y[n]) for n in range(2)))
             return tuple(new)
 
-        zero = jnp.zeros(BLK, F32)
-        sums += list(lax.fori_loop(0, 24, body, tuple((zero, zero) for _ in range(count))))
+        sums += list(
+            lax.fori_loop(0, 24, body, tuple((zero, zero) for _ in range(count)), unroll=2)
+        )
     packed = []
     for first in range(0, len(sums), 8):
         high = low = jnp.zeros(BLK, F32)
@@ -229,11 +253,12 @@
 PAIRS_2 = ((1, 1), (2, 2), (3, 3), (4, 4), (0, 1), (0, 2), (1, 2), (0, 3), (0, 4), (1, 3), (1, 4), (2, 3), (2, 4), (3, 4))
 
 
-def scatter_source(me, n_slabs, weights, slab_of, cell_of, comp_of, source):
+def place_measurements(me, n_slabs, slab_of, cell_of, comp_of, ranks, hot_z, hot_row):
     upper = (iota((LANES, LANES), 0) <= iota((LANES, LANES), 1)).astype(jnp.bfloat16)
     key = (comp_of[...] * 8192 + cell_of[...]).astype(F32)
     n_blocks = key.shape[0]
     slots = n_blocks * CAP
+    same = (iota((slots, slots), 0) == iota((slots, slots), 1)).astype(jnp.bfloat16)
 
     @pl.loop(0, len(SLABS))
     def _(s):
@@ -242,26 +267,36 @@
         mine_f = jnp.where(mine, F32(1), F32(0))
         rank = jnp.dot(mine_f.astype(jnp.bfloat16), upper, preferred_element_type=F32)
         rank = jnp.where(mine, rank, F32(0))
-        slot = (iota((n_blocks, CAP, LANES), 1) + 1).astype(F32)
-        chosen = rank[:, None, :] == slot
-
-        def column(values):
-            v = jnp.where(chosen, values[:, None, :], F32(0))
-            return jnp.sum(v, axis=2, keepdims=True).reshape(slots, 1)
-
-        place = column(key).astype(jnp.int32)
-        hot_z = (place & (LANES - 1)) == iota((slots, LANES), 1)
-        hot_row = jnp.where((place >> 7) == iota((slots, 256), 1), F32(1), F32(0))
+        ranks[s] = rank
+        place = column(rank, key).astype(jnp.int32)
+        at_z = (place & (LANES - 1)) == iota((slots, LANES), 1)
+        hot_z[s] = jnp.where(at_z, F32(1), F32(0))
+        at_row = jnp.where((place >> 7) == iota((slots, 256), 1), F32(1), F32(0))
+        turned = lax.dot_general(
+            at_row.astype(jnp.bfloat16), same, (((0,), (0,)), ((), ())), preferred_element_type=F32
+        )
+        hot_row[s] = turned.astype(jnp.bfloat16)
+
+
+def column(rank, values):
+    n_blocks = rank.shape[0]
+    slot = (iota((n_blocks, CAP, LANES), 1) + 1).astype(F32)
+    v = jnp.where(rank[:, None, :] == slot, values[:, None, :], F32(0))
+    return jnp.sum(v, axis=2, keepdims=True).reshape(n_blocks * CAP, 1)
+
+
+def scatter_source(weights, ranks, hot_z, hot_row, source):
+    @pl.loop(0, len(SLABS))
+    def _(s):
         put = jnp.concatenate(
-            [jnp.where(hot_z, column(weights[:, part, :]), F32(0)) for part in range(2)], axis=1
+            [hot_z[s] * column(ranks[s], weights[:, part, :]) for part in range(2)], axis=1
         )
-        grid = lax.dot_general(
-            hot_row,
-            put,
-            (((0,), (0,)), ((), ())),
-            precision=lax.Precision.HIGHEST,
-            preferred_element_type=F32,
-        )
+        grid = None
+        for _ in range(3):
+            piece = put.astype(jnp.bfloat16)
+            put = put - piece.astype(F32)
+            term = jnp.dot(hot_row[s], piece, preferred_element_type=F32)
+            grid = term if grid is None else grid + term
         for part in range(2):
             for comp in range(3):
                 for plane in range(2):
@@ -271,30 +306,41 @@
                     ]
 
 
+def into(ref):
+    def store(part, comp, at, value):
+        ref[3 * part + comp, at] = value
+
+    return store
+
+
+def place_kernel(
+    n_slabs, slab_of, cell_of, comp_of, freqs, pair, ranks, hot_z, hot_row, wave
+):
+    me = lax.axis_index("space")
+    wave[...] = jnp.full(BLK, freqs[pair[0]], F32)
+    place_measurements(me, n_slabs, slab_of, cell_of, comp_of, ranks, hot_z, hot_row)
+
+
 def start_kernel(
-    n_slabs, own, b2, b1, a1, a2, a3, weights, slab_of, cell_of, comp_of, freqs, pair,
+    own, b2, b1, a1, a2, a3, weights, ranks, hot_z, hot_row, wave,
     p0_out, p1_out, p2_out, damp_out, gram_out,
     field, damping, source, p0, p1,
 ):
     me = lax.axis_index("space")
-    wave = freqs[pair[0]]
     for s, ref in enumerate((b2, b1, own, a1, a2, a3)):
         for k in range(6):
             field[k, 2 * s : 2 * s + 2] = ref[2 * k : 2 * k + 2]
-        damping[2 * s : 2 * s + 2] = ref[12:14] * wave
-    scatter_source(me, n_slabs, weights, slab_of, cell_of, comp_of, source)
+        damping[2 * s : 2 * s + 2] = ref[12:14] * wave[0:1, :]
+    scatter_source(weights, ranks, hot_z, hot_row, source)
 
     def keep_p0(part, comp, at, value):
         p0[3 * part + comp, at] = source[3 * part + comp, at] - value
 
-    def keep_p1(part, comp, at, value):
-        p1[3 * part + comp, at] = value
-
     def keep_p2(part, comp, at, value):
         p2_out[3 * part + comp, at - 3] = value
 
     apply(me, field, damping, -4, 1, 11, keep_p0)
-    apply(me, p0, damping, -4, 2, 10, keep_p1)
+    apply(me, p0, damping, -4, 2, 10, into(p1))
     apply(me, p1, damping, -4, 3, 9, keep_p2)
     for k in range(6):
         p0_out[k] = p0[k, 3:9]
@@ -349,12 +395,6 @@
                 r_out[k] = r[3 * part + c, 1 + plane]
                 m_out[k] = m[3 * part + c, 1 + plane]
 
-    def into(ref):
-        def store(part, comp, at, value):
-            ref[3 * part + comp, at] = value
-
-        return store
-
     apply(me, r, damping, -1, 1, 5, into(f))
     apply(me, m, damping, -1, 2, 4, into(g))
     apply(me, f, damping, -1, 2, 4, into(h))
@@ -363,8 +403,7 @@
     gram(((r, 2), (m, 2), (f, 2), (g, 2), (h, 2)), PAIRS_2, gram_out)
 
 
-def end_kernel(parts, xs, r, d, m, f, background, freqs, pair, adjoint_out, terms_out):
-    wave = freqs[pair[0]]
+def end_kernel(parts, xs, r, d, m, f, background, wave, adjoint_out, terms_out):
     e = gathered(parts, PAIRS_2)
     b = cneg(over(e[1, 2], e[1, 1][0][0]))
     w = [conj(csum([mix(e[i, 1], b), e[i, 2]])) for i in range(5)]
@@ -398,7 +437,7 @@
             adjoint_out[k] = re
             adjoint_out[q] = im
             terms = terms + (re * background[q] + im * background[k])
-        terms = terms * wave
+        terms = terms * wave[0:1, :]
         n_src = terms_out.shape[0]
         part = ROWS // n_src
         for n in range(n_src):
@@ -450,14 +489,29 @@
     comp_of = receiver_component.reshape(n_slabs, LANES)
     smem = spec(pltpu.SMEM)
     six = shaped(6, 6, *plane)
+    slots = n_slabs * CAP
+    places = kernel(
+        functools.partial(place_kernel, n_slabs),
+        "place",
+        [spec()] * 3 + [smem] * 2,
+        [
+            shaped(len(SLABS), *plane),
+            shaped(len(SLABS), slots, LANES),
+            jax.ShapeDtypeStruct((len(SLABS), 256, slots), jnp.bfloat16),
+            shaped(*BLK),
+        ],
+        [],
+        20_000_000,
+    )(slab_of, cell_of, comp_of, frequencies, pair_freq)
+    wave = places[-1]
     p0, p1, p2, damping, parts = kernel(
-        functools.partial(start_kernel, n_slabs),
+        start_kernel,
         "start",
-        [spec()] * 10 + [smem] * 2,
+        [spec()] * 11,
         [six, six, six, shaped(6, *plane), shaped(n_slabs, LANES)],
         [(6, 12, *plane), (12, *plane), (6, 12, *plane), (6, 12, *plane), (6, 12, *plane)],
-        60_000_000,
-    )(message, *window, weights, slab_of, cell_of, comp_of, frequencies, pair_freq)
+        40_000_000,
+    )(message, *window, weights, *places)
     parts = lax.all_to_all(parts, "space", split_axis=0, concat_axis=0, tiled=True)
     two = shaped(12, *plane)
     xs, r, d, m, f, parts = kernel(
@@ -472,11 +526,11 @@
     adjoint, terms = kernel(
         end_kernel,
         "end",
-        [spec()] * 7 + [smem] * 2,
+        [spec()] * 8,
         [two, shaped(n_src, 2 * (ROWS // n_src), LANES)],
         [],
         5_000_000,
-    )(parts, xs, r, d, m, f, background.reshape(12, *plane), frequencies, pair_freq)
+    )(parts, xs, r, d, m, f, background.reshape(12, *plane), wave)
     terms = lax.all_to_all(terms, "src", split_axis=0, concat_axis=0, tiled=True)
     gradient = jnp.sum(terms, axis=0).reshape(2, ROWS // n_src, LANES)
     return adjoint.reshape(warm_start.shape), gradient

time: 84.2 us -> 78.5 us (0.932)
  waiting for transfers between devices: 6.64 us -> 2.6 us
  Pallas kernels: 21.2 us -> 18.9 us
    all_to_all x1, waiting for transfers between devices: 6.63 us -> 2.59 us  [shards(): lax.all_to_all(weights, 'space', split_axis=0, concat_axis=0, tiled=True)]
    pallas_call x1, Pallas kernels: 7.8 us -> 5.52 us  [shards(): kernel(middle_kernel, 'middle', [spec()] * 6, [two] * 5 + [shaped(n_slabs...]
    pallas_call x2 -> x3, Pallas kernels: 13.4 us -> 13.4 us  [the longest x1 8.55 us: shards(): kernel(start_kernel, 'start', [spec()] * 11, [six, six, six, shaped(6, *p...]
  transfers between devices with their start and end apart: 6 -> 6, of which waited for: 1 -> 1; matrix products, arithmetic and copies ran while one was open for 1% -> 1% of each run, Pallas kernels for 0% -> 4%
where the time goes in v2:
time: 78.5 us; the launch traced here: 78.1 us
  blocking collectives  37.1 us (47%)
  Pallas kernels  18.9 us (24%)
  starting transfers between devices  15.3 us (19%)
  waiting for transfers between devices  2.6 us (3%)
  other arithmetic  1.57 us (2%)
  between operations  1.37 us (2%)
  local copies, waits for them, and re-layouts  1.27 us (2%)
    all_to_all x2, blocking collectives, shards(): lax.all_to_all(parts, 'space', split_axis=0, concat_axis=0, tiled=True)  22.2 us
    all_to_all x1, blocking collectives, shards(): lax.all_to_all(terms, 'src', split_axis=0, concat_axis=0, tiled=True)  14.8 us
    ppermute x5, starting transfers between devices, from_slab(): return lax.ppermute(message, 'space', route)  9.61 us
    pallas_call x1, Pallas kernels, shards(): kernel(start_kernel, 'start', [spec()] * 11, [six, six, six, shaped(6, *p...  8.55 us
    all_to_all x1, starting transfers between devices, shards(): lax.all_to_all(weights, 'space', split_axis=0, concat_axis=0, tiled=True)  5.74 us
    pallas_call x1, Pallas kernels, shards(): kernel(middle_kernel, 'middle', [spec()] * 6, [two] * 5 + [shaped(n_slabs...  5.52 us
    pallas_call x1, Pallas kernels, shards(): kernel(functools.partial(place_kernel, n_slabs), 'place', [spec()] * 3 +...  3.37 us
    all_to_all x1, waiting for transfers between devices, shards(): lax.all_to_all(weights, 'space', split_axis=0, concat_axis=0, tiled=True)  2.59 us
  transfers between devices with their start and end apart: 6, of which 1 were waited for; matrix products, arithmetic and copies ran while one was open for 1% of the time, Pallas kernels for 4%

profile of v2, /device:TPU:1, one launch (start us, length us, event | category | flops | bytes accessed | tf_op | source)
XLA Modules:
  0.0 78.1 jit_solution(2227530598180948936)
XLA Ops:
  0.6 1.0 %pad_maximum_fusion.own = f32[14,32,128]{2,1,0:T(8,128)S(1)} fusion(f32[2,32,128]{2,1,0:T(8,128)} %param.11, f32[12,32,128]{2,1,0:T(8,128)} %bitcast.18), kind=kLoop, calls=%fused_computation | loop fusion | flops 57344 | bytes 458752 | tf_op jit(solution)/shard_map/concatenate | solution.py:477
  1.6 0.0 copy-start.6
  1.6 6.4 %collective-permute-start.4 = (f32[14,32,128]{2,1,0:T(8,128)S(1)}, f32[14,32,128]{2,1,0:T(8,128)S(1)}, u32[]{:S(2)}, u32[]{:S(2)}) collective-permute-start(f32[14,32,128]{2,1,0:T(8,128)S(1)} %pad_maximum_fusion.own), channel_id=1, source_target_pairs={{3,0},{4,1},{5,2},{6,3},{7,4},{8,5},{9,6},{10,7},{11,8},{12,9},{13... | collective-permute-start | bytes 688136 | tf_op jit(solution)/shard_map/ppermute | solution.py:481
  8.0 0.5 collective-permute-start.3
  8.5 0.6 collective-permute-start.2
  9.1 1.1 %collective-permute-start.1 = (f32[14,32,128]{2,1,0:T(8,128)S(1)}, f32[14,32,128]{2,1,0:T(8,128)S(1)}, u32[]{:S(2)}, u32[]{:S(2)}) collective-permute-start(f32[14,32,128]{2,1,0:T(8,128)S(1)} %pad_maximum_fusion.own), channel_id=1, source_target_pairs={{31,0},{0,1},{1,2},{2,3},{3,4},{4,5},{5,6},{6,7},{7,8},{8,9},{9,10... | collective-permute-start | bytes 688136 | tf_op jit(solution)/shard_map/ppermute | solution.py:481
  10.2 1.0 %collective-permute-start = (f32[14,32,128]{2,1,0:T(8,128)S(1)}, f32[14,32,128]{2,1,0:T(8,128)S(1)}, u32[]{:S(2)}, u32[]{:S(2)}) collective-permute-start(f32[14,32,128]{2,1,0:T(8,128)S(1)} %pad_maximum_fusion.own), channel_id=1, source_target_pairs={{30,0},{31,1},{0,2},{1,3},{2,4},{3,5},{4,6},{5,7},{6,8},{7,9},{8,1... | collective-permute-start | bytes 688136 | tf_op jit(solution)/shard_map/ppermute | solution.py:481
  11.2 0.0 copy-done.6
  11.2 0.6 broadcast_in_dim.8
  11.8 0.0 copy-start.2
  11.8 0.0 copy-start.3
  11.8 0.0 copy-start.4
  11.9 5.7 %all-to-all-start = ((f32[32,2,128]{2,1,0:T(2,128)}), f32[32,2,128]{2,1,0:T(2,128)S(1)}, u32[]{:S(2)}, u32[]{:S(2)}) async-start(f32[32,2,128]{2,1,0:T(2,128)} %broadcast_in_dim.8), calls=%async_computation | async-start | bytes 65536 | tf_op jit(solution)/shard_map/all_to_all | solution.py:485
  18.2 0.0 copy-start.5
  18.3 0.0 copy-done.2
  18.3 0.0 copy-done.3
  18.3 0.0 copy-done.4
  18.3 0.6 copy-done.5
  18.9 3.4 %place.1 = (f32[6,32,128]{2,1,0:T(8,128)S(1)}, f32[6,256,128]{2,1,0:T(8,128)S(1)}, bf16[6,256,256]{2,1,0:T(8,128)(2,1)S(1)}, f32[8,128]{1,0:T(8,128)S(1)}) custom-call(s32[32,128]{1,0:T(8,128)S(1)} %bitcast.25, s32[32,128]{1,0:T(8,128)S(1)} %bitcast.26, s32[32,128]{1,0:T(8,128)S(1)} %bitcast.27, f32[8]{0:T(128)S(1)} %copy-done.5, s32[1]{0:T(128)S(6)} %copy.15.pair), custom_call_target="tpu_custom_call" | custom-call | flops 20000000 | bytes 3000000 | tf_op jit(solution)/shard_map/place/pallas_call | solution.py:493
  22.3 2.6 %all-to-all-done.weights = f32[32,2,128]{2,1,0:T(2,128)S(1)} async-done(((f32[32,2,128]{2,1,0:T(2,128)}), f32[32,2,128]{2,1,0:T(2,128)S(1)}, u32[]{:S(2)}, u32[]{:S(2)}) %all-to-all-start) | async-done | bytes 32800 | tf_op jit(solution)/shard_map/all_to_all | solution.py:485
  24.9 0.0 collective-permute-done.4.a3
  24.9 0.0 collective-permute-done.3.a2
  24.9 0.0 collective-permute-done.2.a1
  24.9 0.0 collective-permute-done.1.b1
  24.9 0.0 collective-permute-done.b2
  24.9 0.0 copy-start
  24.9 8.6 %start.1 = (f32[6,6,32,128]{3,2,1,0:T(8,128)S(1)}, f32[6,6,32,128]{3,2,1,0:T(8,128)S(1)}, f32[6,6,32,128]{3,2,1,0:T(8,128)S(1)}, f32[6,32,128]{2,1,0:T(8,128)S(1)}, f32[32,128]{1,0:T(8,128)S(1)}) custom-call(f32[14,32,128]{2,1,0:T(8,128)S(1)} %pad_maximum_fusion.own, f32[14,32,128]{2,1,0:T(8,128)S(1)} %collective-permute-done.b2, ...), custom_call_target="tpu_custom_call" | custom-call | flops 40000000 | bytes 3000000 | tf_op jit(solution)/shard_map/start/pallas_call | solution.py:507
  33.5 11.6 %all_to_all.32 = f32[32,1,128]{2,1,0:T(1,128)S(1)} all-to-all(f32[32,1,128]{2,1,0:T(1,128)S(1)} %bitcast.23), channel_id=1, replica_groups=mesh['src'=8,'space'=32] {'space'}, dimensions={0} | all-to-all | bytes 32768 | tf_op jit(solution)/shard_map/all_to_all | solution.py:515
  45.0 0.0 copy-done
  45.0 0.0 copy-start.1
  45.0 5.5 %middle.1 = (f32[12,32,128]{2,1,0:T(8,128)S(1)}, f32[12,32,128]{2,1,0:T(8,128)S(1)}, f32[12,32,128]{2,1,0:T(8,128)S(1)}, f32[12,32,128]{2,1,0:T(8,128)S(1)}, f32...) custom-call(f32[32,128]{1,0:T(8,128)S(1)} %bitcast.21, f32[6,6,32,128]{3,2,1,0:T(8,128)S(1)} %get-tuple-element.24.p0, ...), custom_call_target="tpu_custom_call" | custom-call | flops 40000000 | bytes 3000000 | tf_op jit(solution)/shard_map/middle/pallas_call | solution.py:517
  50.6 10.7 %all_to_all.33 = f32[32,1,128]{2,1,0:T(1,128)S(1)} all-to-all(f32[32,1,128]{2,1,0:T(1,128)S(1)} %bitcast.24), channel_id=1, replica_groups=mesh['src'=8,'space'=32] {'space'}, dimensions={0} | all-to-all | bytes 32768 | tf_op jit(solution)/shard_map/all_to_all | solution.py:525
  61.2 0.0 copy-done.1
  61.2 1.5 %end.1 = (f32[12,32,128]{2,1,0:T(8,128)}, f32[8,8,128]{2,1,0:T(8,128)S(1)}) custom-call(f32[32,128]{1,0:T(8,128)S(1)} %bitcast.22, f32[12,32,128]{2,1,0:T(8,128)S(1)} %get-tuple-element.29.xs, f32[12,32,128]{2,1,0:T(8,128)S(1)} %get-tuple-element.30.r, f32[12,32,128]{2,1,0:T(8,128)S(1)} %get-tuple-element.31.d, f32[12,32,128]{2,1,0:T(8,128)S(1)} %get-tuple-element.32.m, ...), custom_call_target="tpu_custom_call" | custom-call | flops 5000000 | bytes 3000000 | tf_op jit(solution)/shard_map/end/pallas_call | solution.py:526
  62.7 14.8 %all_to_all.34 = f32[8,8,128]{2,1,0:T(8,128)S(1)} all-to-all(f32[8,8,128]{2,1,0:T(8,128)S(1)} %get-tuple-element.35), channel_id=1, replica_groups=mesh['src'=8,'space'=32] {'src'}, dimensions={0} | all-to-all | bytes 65536 | tf_op jit(solution)/shard_map/all_to_all | solution.py:534
  77.5 0.6 reduce_sum.9
Async XLA Ops:
  1.6 9.6 %copy-start.6 = (f32[2,1,128]{2,1,0:T(1,128)S(1)}, f32[2,1,128]{2,1,0:T(1,128)}, u32[]{:S(2)}) copy-start(f32[2,1,128]{2,1,0:T(1,128)} %param.14) | copy-start | bytes 3076
  1.6 23.3 %collective-permute-start.4 = (f32[14,32,128]{2,1,0:T(8,128)S(1)}, f32[14,32,128]{2,1,0:T(8,128)S(1)}, u32[]{:S(2)}, u32[]{:S(2)}) collective-permute-start(f32[14,32,128]{2,1,0:T(8,128)S(1)} %pad_maximum_fusion.own), channel_id=1, source_target_pairs={{3,0},{4,1},{5,2},{6,3},{7,4},{8,5},{9,6},{10,7},{11,8},{12,9},{13... | collective-permute-start | bytes 688136 | tf_op jit(solution)/shard_map/ppermute | solution.py:481
  8.0 16.9 %collective-permute-start.3 = (f32[14,32,128]{2,1,0:T(8,128)S(1)}, f32[14,32,128]{2,1,0:T(8,128)S(1)}, u32[]{:S(2)}, u32[]{:S(2)}) collective-permute-start(f32[14,32,128]{2,1,0:T(8,128)S(1)} %pad_maximum_fusion.own), channel_id=1, source_target_pairs={{2,0},{3,1},{4,2},{5,3},{6,4},{7,5},{8,6},{9,7},{10,8},{11,9},{12,... | collective-permute-start | bytes 688136 | tf_op jit(solution)/shard_map/ppermute | solution.py:481
  8.5 16.4 %collective-permute-start.2 = (f32[14,32,128]{2,1,0:T(8,128)S(1)}, f32[14,32,128]{2,1,0:T(8,128)S(1)}, u32[]{:S(2)}, u32[]{:S(2)}) collective-permute-start(f32[14,32,128]{2,1,0:T(8,128)S(1)} %pad_maximum_fusion.own), channel_id=1, source_target_pairs={{1,0},{2,1},{3,2},{4,3},{5,4},{6,5},{7,6},{8,7},{9,8},{10,9},{11,1... | collective-permute-start | bytes 688136 | tf_op jit(solution)/shard_map/ppermute | solution.py:481
  9.1 15.8 %collective-permute-start.1 = (f32[14,32,128]{2,1,0:T(8,128)S(1)}, f32[14,32,128]{2,1,0:T(8,128)S(1)}, u32[]{:S(2)}, u32[]{:S(2)}) collective-permute-start(f32[14,32,128]{2,1,0:T(8,128)S(1)} %pad_maximum_fusion.own), channel_id=1, source_target_pairs={{31,0},{0,1},{1,2},{2,3},{3,4},{4,5},{5,6},{6,7},{7,8},{8,9},{9,10... | collective-permute-start | bytes 688136 | tf_op jit(solution)/shard_map/ppermute | solution.py:481
  10.2 14.7 %collective-permute-start = (f32[14,32,128]{2,1,0:T(8,128)S(1)}, f32[14,32,128]{2,1,0:T(8,128)S(1)}, u32[]{:S(2)}, u32[]{:S(2)}) collective-permute-start(f32[14,32,128]{2,1,0:T(8,128)S(1)} %pad_maximum_fusion.own), channel_id=1, source_target_pairs={{30,0},{31,1},{0,2},{1,3},{2,4},{3,5},{4,6},{5,7},{6,8},{7,9},{8,1... | collective-permute-start | bytes 688136 | tf_op jit(solution)/shard_map/ppermute | solution.py:481
  11.8 6.4 %copy-start.2 = (s32[4096,1]{0,1:T(1,128)S(1)}, s32[4096,1]{0,1:T(1,128)}, u32[]{:S(2)}) copy-start(s32[4096,1]{0,1:T(1,128)} %param.15) | copy-start | bytes 49156
  11.8 6.4 %copy-start.3 = (s32[4096]{0:T(1024)S(1)}, s32[4096]{0:T(1024)}, u32[]{:S(2)}) copy-start(s32[4096]{0:T(1024)} %param.16) | copy-start | bytes 49156
  11.8 6.4 %copy-start.4 = (s32[4096]{0:T(1024)S(1)}, s32[4096]{0:T(1024)}, u32[]{:S(2)}) copy-start(s32[4096]{0:T(1024)} %param.17) | copy-start | bytes 49156
  11.9 13.0 %all-to-all-start = ((f32[32,2,128]{2,1,0:T(2,128)}), f32[32,2,128]{2,1,0:T(2,128)S(1)}, u32[]{:S(2)}, u32[]{:S(2)}) async-start(f32[32,2,128]{2,1,0:T(2,128)} %broadcast_in_dim.8), calls=%async_computation | async-start | bytes 65536 | tf_op jit(solution)/shard_map/all_to_all | solution.py:485
  18.2 0.7 copy-start.5
  24.9 20.1 %copy-start = (f32[2,1,3,2,32,128]{5,4,3,2,1,0:T(8,128)S(1)}, f32[2,1,3,2,32,128]{5,4,3,2,1,0:T(8,128)}, u32[]{:S(2)}) copy-start(f32[2,1,3,2,32,128]{5,4,3,2,1,0:T(8,128)} %param.10) | copy-start | bytes 589828
  45.0 16.2 %copy-start.1 = (f32[2,1,3,2,32,128]{5,4,3,2,1,0:T(8,128)S(1)}, f32[2,1,3,2,32,128]{5,4,3,2,1,0:T(8,128)}, u32[]{:S(2)}) copy-start(f32[2,1,3,2,32,128]{5,4,3,2,1,0:T(8,128)} %param.9) | copy-start | bytes 589828

commit v3 on v2

--- a/solution.py
+++ b/solution.py
@@ -128,7 +128,7 @@
     return result, (hy, hz)
 
 
-def apply(me, field, damping, first, low, high, store):
+def apply(me, field, damping, first, low, high, store, unroll=2):
     def plane(at, before):
         grid_plane = lax.rem(2 * me + first + at + 64, 64)
         above = jnp.where(grid_plane == 63, F32(0), F32(1))
@@ -146,10 +146,10 @@
     for part in range(2):
         under = [field[3 * part + c, low - 1] for c in range(3)]
         below_first += forward_yz(*under, *(field[3 * part + c, low] for c in (1, 2)))
-    lax.fori_loop(low, high, plane, tuple(below_first))
-
-
-def gram(fields, pairs, out, size=4):
+    lax.fori_loop(low, high, plane, tuple(below_first), unroll=unroll)
+
+
+def gram(fields, pairs, out, size=14):
     names = sorted({k for pair in pairs for k in pair})
 
     def block(step, k, part):
@@ -196,7 +196,7 @@
             return tuple(new)
 
         sums += list(
-            lax.fori_loop(0, 24, body, tuple((zero, zero) for _ in range(count)), unroll=2)
+            lax.fori_loop(0, 24, body, tuple((zero, zero) for _ in range(count)), unroll=4)
         )
     packed = []
     for first in range(0, len(sums), 8):
@@ -286,7 +286,7 @@
 
 
 def scatter_source(weights, ranks, hot_z, hot_row, source):
-    @pl.loop(0, len(SLABS))
+    @pl.loop(0, len(SLABS), unroll=len(SLABS))
     def _(s):
         put = jnp.concatenate(
             [hot_z[s] * column(ranks[s], weights[:, part, :]) for part in range(2)], axis=1
@@ -339,9 +339,9 @@
     def keep_p2(part, comp, at, value):
         p2_out[3 * part + comp, at - 3] = value
 
-    apply(me, field, damping, -4, 1, 11, keep_p0)
-    apply(me, p0, damping, -4, 2, 10, into(p1))
-    apply(me, p1, damping, -4, 3, 9, keep_p2)
+    apply(me, field, damping, -4, 1, 11, keep_p0, 5)
+    apply(me, p0, damping, -4, 2, 10, into(p1), 4)
+    apply(me, p1, damping, -4, 3, 9, keep_p2, 3)
     for k in range(6):
         p0_out[k] = p0[k, 3:9]
         p1_out[k] = p1[k, 3:9]

time: 78.5 us -> 72.6 us (0.925)
  Pallas kernels: 18.9 us -> 13 us
    pallas_call x1, Pallas kernels: 8.55 us -> 4.49 us  [shards(): kernel(start_kernel, 'start', [spec()] * 11, [six, six, six, shaped(6, *p...]
    pallas_call x1, Pallas kernels: 5.52 us -> 3.69 us  [shards(): kernel(middle_kernel, 'middle', [spec()] * 6, [two] * 5 + [shaped(n_slabs...]
  transfers between devices with their start and end apart: 6 -> 6, of which waited for: 1 -> 1; matrix products, arithmetic and copies ran while one was open for 1% -> 1% of each run, Pallas kernels for 4% -> 5%
where the time goes in v3:
time: 72.6 us; the launch traced here: 72.2 us
  blocking collectives  37.1 us (51%)
  starting transfers between devices  15.3 us (21%)
  Pallas kernels  13 us (18%)
  waiting for transfers between devices  2.6 us (4%)
  other arithmetic  1.57 us (2%)
  between operations  1.37 us (2%)
  local copies, waits for them, and re-layouts  1.27 us (2%)
    all_to_all x2, blocking collectives, shards(): lax.all_to_all(parts, 'space', split_axis=0, concat_axis=0, tiled=True)  22.2 us
    all_to_all x1, blocking collectives, shards(): lax.all_to_all(terms, 'src', split_axis=0, concat_axis=0, tiled=True)  14.8 us
    ppermute x5, starting transfers between devices, from_slab(): return lax.ppermute(message, 'space', route)  9.61 us
    all_to_all x1, starting transfers between devices, shards(): lax.all_to_all(weights, 'space', split_axis=0, concat_axis=0, tiled=True)  5.74 us
    pallas_call x1, Pallas kernels, shards(): kernel(start_kernel, 'start', [spec()] * 11, [six, six, six, shaped(6, *p...  4.49 us
    pallas_call x1, Pallas kernels, shards(): kernel(middle_kernel, 'middle', [spec()] * 6, [two] * 5 + [shaped(n_slabs...  3.69 us
    pallas_call x1, Pallas kernels, shards(): kernel(functools.partial(place_kernel, n_slabs), 'place', [spec()] * 3 +...  3.37 us
    all_to_all x1, waiting for transfers between devices, shards(): lax.all_to_all(weights, 'space', split_axis=0, concat_axis=0, tiled=True)  2.59 us
  transfers between devices with their start and end apart: 6, of which 1 were waited for; matrix products, arithmetic and copies ran while one was open for 1% of the time, Pallas kernels for 5%

profile of v3, /device:TPU:1, one launch (start us, length us, event | category | flops | bytes accessed | tf_op | source)
XLA Modules:
  0.0 72.2 jit_solution(3325783433902125782)
XLA Ops:
  0.6 1.0 %pad_maximum_fusion.own = f32[14,32,128]{2,1,0:T(8,128)S(1)} fusion(f32[2,32,128]{2,1,0:T(8,128)} %param.11, f32[12,32,128]{2,1,0:T(8,128)} %bitcast.18), kind=kLoop, calls=%fused_computation | loop fusion | flops 57344 | bytes 458752 | tf_op jit(solution)/shard_map/concatenate | solution.py:477
  1.6 0.0 copy-start.6
  1.6 6.4 %collective-permute-start.4 = (f32[14,32,128]{2,1,0:T(8,128)S(1)}, f32[14,32,128]{2,1,0:T(8,128)S(1)}, u32[]{:S(2)}, u32[]{:S(2)}) collective-permute-start(f32[14,32,128]{2,1,0:T(8,128)S(1)} %pad_maximum_fusion.own), channel_id=1, source_target_pairs={{3,0},{4,1},{5,2},{6,3},{7,4},{8,5},{9,6},{10,7},{11,8},{12,9},{13... | collective-permute-start | bytes 688136 | tf_op jit(solution)/shard_map/ppermute | solution.py:481
  8.0 0.5 collective-permute-start.3
  8.5 0.6 collective-permute-start.2
  9.1 1.1 %collective-permute-start.1 = (f32[14,32,128]{2,1,0:T(8,128)S(1)}, f32[14,32,128]{2,1,0:T(8,128)S(1)}, u32[]{:S(2)}, u32[]{:S(2)}) collective-permute-start(f32[14,32,128]{2,1,0:T(8,128)S(1)} %pad_maximum_fusion.own), channel_id=1, source_target_pairs={{31,0},{0,1},{1,2},{2,3},{3,4},{4,5},{5,6},{6,7},{7,8},{8,9},{9,10... | collective-permute-start | bytes 688136 | tf_op jit(solution)/shard_map/ppermute | solution.py:481
  10.2 1.0 %collective-permute-start = (f32[14,32,128]{2,1,0:T(8,128)S(1)}, f32[14,32,128]{2,1,0:T(8,128)S(1)}, u32[]{:S(2)}, u32[]{:S(2)}) collective-permute-start(f32[14,32,128]{2,1,0:T(8,128)S(1)} %pad_maximum_fusion.own), channel_id=1, source_target_pairs={{30,0},{31,1},{0,2},{1,3},{2,4},{3,5},{4,6},{5,7},{6,8},{7,9},{8,1... | collective-permute-start | bytes 688136 | tf_op jit(solution)/shard_map/ppermute | solution.py:481
  11.2 0.0 copy-done.6
  11.2 0.6 broadcast_in_dim.8
  11.8 0.0 copy-start.2
  11.8 0.0 copy-start.3
  11.8 0.0 copy-start.4
  11.9 5.7 %all-to-all-start = ((f32[32,2,128]{2,1,0:T(2,128)}), f32[32,2,128]{2,1,0:T(2,128)S(1)}, u32[]{:S(2)}, u32[]{:S(2)}) async-start(f32[32,2,128]{2,1,0:T(2,128)} %broadcast_in_dim.8), calls=%async_computation | async-start | bytes 65536 | tf_op jit(solution)/shard_map/all_to_all | solution.py:485
  18.2 0.0 copy-start.5
  18.3 0.0 copy-done.2
  18.3 0.0 copy-done.3
  18.3 0.0 copy-done.4
  18.3 0.6 copy-done.5
  18.9 3.4 %place.1 = (f32[6,32,128]{2,1,0:T(8,128)S(1)}, f32[6,256,128]{2,1,0:T(8,128)S(1)}, bf16[6,256,256]{2,1,0:T(8,128)(2,1)S(1)}, f32[8,128]{1,0:T(8,128)S(1)}) custom-call(s32[32,128]{1,0:T(8,128)S(1)} %bitcast.25, s32[32,128]{1,0:T(8,128)S(1)} %bitcast.26, s32[32,128]{1,0:T(8,128)S(1)} %bitcast.27, f32[8]{0:T(128)S(1)} %copy-done.5, s32[1]{0:T(128)S(6)} %copy.15.pair), custom_call_target="tpu_custom_call" | custom-call | flops 20000000 | bytes 3000000 | tf_op jit(solution)/shard_map/place/pallas_call | solution.py:493
  22.3 2.6 %all-to-all-done.weights = f32[32,2,128]{2,1,0:T(2,128)S(1)} async-done(((f32[32,2,128]{2,1,0:T(2,128)}), f32[32,2,128]{2,1,0:T(2,128)S(1)}, u32[]{:S(2)}, u32[]{:S(2)}) %all-to-all-start) | async-done | bytes 32800 | tf_op jit(solution)/shard_map/all_to_all | solution.py:485
  24.9 0.0 collective-permute-done.4.a3
  24.9 0.0 collective-permute-done.3.a2
  24.9 0.0 collective-permute-done.2.a1
  24.9 0.0 collective-permute-done.1.b1
  24.9 0.0 collective-permute-done.b2
  24.9 0.0 copy-start
  24.9 4.5 %start.1 = (f32[6,6,32,128]{3,2,1,0:T(8,128)S(1)}, f32[6,6,32,128]{3,2,1,0:T(8,128)S(1)}, f32[6,6,32,128]{3,2,1,0:T(8,128)S(1)}, f32[6,32,128]{2,1,0:T(8,128)S(1)}, f32[32,128]{1,0:T(8,128)S(1)}) custom-call(f32[14,32,128]{2,1,0:T(8,128)S(1)} %pad_maximum_fusion.own, f32[14,32,128]{2,1,0:T(8,128)S(1)} %collective-permute-done.b2, ...), custom_call_target="tpu_custom_call" | custom-call | flops 40000000 | bytes 3000000 | tf_op jit(solution)/shard_map/start/pallas_call | solution.py:507
  29.4 11.6 %all_to_all.32 = f32[32,1,128]{2,1,0:T(1,128)S(1)} all-to-all(f32[32,1,128]{2,1,0:T(1,128)S(1)} %bitcast.23), channel_id=1, replica_groups=mesh['src'=8,'space'=32] {'space'}, dimensions={0} | all-to-all | bytes 32768 | tf_op jit(solution)/shard_map/all_to_all | solution.py:515
  41.0 0.0 copy-done
  41.0 0.0 copy-start.1
  41.0 3.7 %middle.1 = (f32[12,32,128]{2,1,0:T(8,128)S(1)}, f32[12,32,128]{2,1,0:T(8,128)S(1)}, f32[12,32,128]{2,1,0:T(8,128)S(1)}, f32[12,32,128]{2,1,0:T(8,128)S(1)}, f32...) custom-call(f32[32,128]{1,0:T(8,128)S(1)} %bitcast.21, f32[6,6,32,128]{3,2,1,0:T(8,128)S(1)} %get-tuple-element.24.p0, ...), custom_call_target="tpu_custom_call" | custom-call | flops 40000000 | bytes 3000000 | tf_op jit(solution)/shard_map/middle/pallas_call | solution.py:517
  44.7 10.7 %all_to_all.33 = f32[32,1,128]{2,1,0:T(1,128)S(1)} all-to-all(f32[32,1,128]{2,1,0:T(1,128)S(1)} %bitcast.24), channel_id=1, replica_groups=mesh['src'=8,'space'=32] {'space'}, dimensions={0} | all-to-all | bytes 32768 | tf_op jit(solution)/shard_map/all_to_all | solution.py:525
  55.3 0.0 copy-done.1
  55.3 1.5 %end.1 = (f32[12,32,128]{2,1,0:T(8,128)}, f32[8,8,128]{2,1,0:T(8,128)S(1)}) custom-call(f32[32,128]{1,0:T(8,128)S(1)} %bitcast.22, f32[12,32,128]{2,1,0:T(8,128)S(1)} %get-tuple-element.29.xs, f32[12,32,128]{2,1,0:T(8,128)S(1)} %get-tuple-element.30.r, f32[12,32,128]{2,1,0:T(8,128)S(1)} %get-tuple-element.31.d, f32[12,32,128]{2,1,0:T(8,128)S(1)} %get-tuple-element.32.m, ...), custom_call_target="tpu_custom_call" | custom-call | flops 5000000 | bytes 3000000 | tf_op jit(solution)/shard_map/end/pallas_call | solution.py:526
  56.8 14.8 %all_to_all.34 = f32[8,8,128]{2,1,0:T(8,128)S(1)} all-to-all(f32[8,8,128]{2,1,0:T(8,128)S(1)} %get-tuple-element.35), channel_id=1, replica_groups=mesh['src'=8,'space'=32] {'src'}, dimensions={0} | all-to-all | bytes 65536 | tf_op jit(solution)/shard_map/all_to_all | solution.py:534
  71.6 0.6 reduce_sum.9
Async XLA Ops:
  1.6 9.6 %copy-start.6 = (f32[2,1,128]{2,1,0:T(1,128)S(1)}, f32[2,1,128]{2,1,0:T(1,128)}, u32[]{:S(2)}) copy-start(f32[2,1,128]{2,1,0:T(1,128)} %param.14) | copy-start | bytes 3076
  1.6 23.3 %collective-permute-start.4 = (f32[14,32,128]{2,1,0:T(8,128)S(1)}, f32[14,32,128]{2,1,0:T(8,128)S(1)}, u32[]{:S(2)}, u32[]{:S(2)}) collective-permute-start(f32[14,32,128]{2,1,0:T(8,128)S(1)} %pad_maximum_fusion.own), channel_id=1, source_target_pairs={{3,0},{4,1},{5,2},{6,3},{7,4},{8,5},{9,6},{10,7},{11,8},{12,9},{13... | collective-permute-start | bytes 688136 | tf_op jit(solution)/shard_map/ppermute | solution.py:481
  8.0 16.9 %collective-permute-start.3 = (f32[14,32,128]{2,1,0:T(8,128)S(1)}, f32[14,32,128]{2,1,0:T(8,128)S(1)}, u32[]{:S(2)}, u32[]{:S(2)}) collective-permute-start(f32[14,32,128]{2,1,0:T(8,128)S(1)} %pad_maximum_fusion.own), channel_id=1, source_target_pairs={{2,0},{3,1},{4,2},{5,3},{6,4},{7,5},{8,6},{9,7},{10,8},{11,9},{12,... | collective-permute-start | bytes 688136 | tf_op jit(solution)/shard_map/ppermute | solution.py:481
  8.5 16.4 %collective-permute-start.2 = (f32[14,32,128]{2,1,0:T(8,128)S(1)}, f32[14,32,128]{2,1,0:T(8,128)S(1)}, u32[]{:S(2)}, u32[]{:S(2)}) collective-permute-start(f32[14,32,128]{2,1,0:T(8,128)S(1)} %pad_maximum_fusion.own), channel_id=1, source_target_pairs={{1,0},{2,1},{3,2},{4,3},{5,4},{6,5},{7,6},{8,7},{9,8},{10,9},{11,1... | collective-permute-start | bytes 688136 | tf_op jit(solution)/shard_map/ppermute | solution.py:481
  9.1 15.8 %collective-permute-start.1 = (f32[14,32,128]{2,1,0:T(8,128)S(1)}, f32[14,32,128]{2,1,0:T(8,128)S(1)}, u32[]{:S(2)}, u32[]{:S(2)}) collective-permute-start(f32[14,32,128]{2,1,0:T(8,128)S(1)} %pad_maximum_fusion.own), channel_id=1, source_target_pairs={{31,0},{0,1},{1,2},{2,3},{3,4},{4,5},{5,6},{6,7},{7,8},{8,9},{9,10... | collective-permute-start | bytes 688136 | tf_op jit(solution)/shard_map/ppermute | solution.py:481
  10.2 14.7 %collective-permute-start = (f32[14,32,128]{2,1,0:T(8,128)S(1)}, f32[14,32,128]{2,1,0:T(8,128)S(1)}, u32[]{:S(2)}, u32[]{:S(2)}) collective-permute-start(f32[14,32,128]{2,1,0:T(8,128)S(1)} %pad_maximum_fusion.own), channel_id=1, source_target_pairs={{30,0},{31,1},{0,2},{1,3},{2,4},{3,5},{4,6},{5,7},{6,8},{7,9},{8,1... | collective-permute-start | bytes 688136 | tf_op jit(solution)/shard_map/ppermute | solution.py:481
  11.8 6.4 %copy-start.2 = (s32[4096,1]{0,1:T(1,128)S(1)}, s32[4096,1]{0,1:T(1,128)}, u32[]{:S(2)}) copy-start(s32[4096,1]{0,1:T(1,128)} %param.15) | copy-start | bytes 49156
  11.8 6.4 %copy-start.3 = (s32[4096]{0:T(1024)S(1)}, s32[4096]{0:T(1024)}, u32[]{:S(2)}) copy-start(s32[4096]{0:T(1024)} %param.16) | copy-start | bytes 49156
  11.8 6.4 %copy-start.4 = (s32[4096]{0:T(1024)S(1)}, s32[4096]{0:T(1024)}, u32[]{:S(2)}) copy-start(s32[4096]{0:T(1024)} %param.17) | copy-start | bytes 49156
  11.9 13.0 %all-to-all-start = ((f32[32,2,128]{2,1,0:T(2,128)}), f32[32,2,128]{2,1,0:T(2,128)S(1)}, u32[]{:S(2)}, u32[]{:S(2)}) async-start(f32[32,2,128]{2,1,0:T(2,128)} %broadcast_in_dim.8), calls=%async_computation | async-start | bytes 65536 | tf_op jit(solution)/shard_map/all_to_all | solution.py:485
  18.2 0.7 copy-start.5
  24.9 16.1 %copy-start = (f32[2,1,3,2,32,128]{5,4,3,2,1,0:T(8,128)S(1)}, f32[2,1,3,2,32,128]{5,4,3,2,1,0:T(8,128)}, u32[]{:S(2)}) copy-start(f32[2,1,3,2,32,128]{5,4,3,2,1,0:T(8,128)} %param.10) | copy-start | bytes 589828
  41.0 14.4 %copy-start.1 = (f32[2,1,3,2,32,128]{5,4,3,2,1,0:T(8,128)S(1)}, f32[2,1,3,2,32,128]{5,4,3,2,1,0:T(8,128)}, u32[]{:S(2)}) copy-start(f32[2,1,3,2,32,128]{5,4,3,2,1,0:T(8,128)} %param.9) | copy-start | bytes 589828

commit v4 on v3

--- a/solution.py
+++ b/solution.py
@@ -149,7 +149,7 @@
     lax.fori_loop(low, high, plane, tuple(below_first), unroll=unroll)
 
 
-def gram(fields, pairs, out, size=14):
+def gram(fields, pairs, out, spare, size=14):
     names = sorted({k for pair in pairs for k in pair})
 
     def block(step, k, part):
@@ -165,7 +165,7 @@
         )
 
     zero = jnp.zeros(BLK, F32)
-    tops = lax.fori_loop(0, 24, peak, tuple(zero for _ in names), unroll=2)
+    tops = lax.fori_loop(0, 24, peak, tuple(zero for _ in names), unroll=6)
     grids = {k: top * F32(2.0**15) for k, top in zip(names, tops)}
     sums = []
     for first in range(0, len(pairs), size):
@@ -196,23 +196,20 @@
             return tuple(new)
 
         sums += list(
-            lax.fori_loop(0, 24, body, tuple((zero, zero) for _ in range(count)), unroll=4)
+            lax.fori_loop(0, 24, body, tuple((zero, zero) for _ in range(count)), unroll=6)
         )
-    packed = []
-    for first in range(0, len(sums), 8):
-        high = low = jnp.zeros(BLK, F32)
-        for k, s in enumerate(sums[first : first + 8]):
-            for shift in (4, 2, 1):
-                s = pair_add(s, tuple(pltpu.roll(v, shift, 0) for v in s))
-            here = iota(BLK, 0) == k
-            high, low = jnp.where(here, s[0], high), jnp.where(here, s[1], low)
-        packed.append((high, low))
-    line = jnp.zeros(BLK, F32)
-    for n, s in enumerate(packed):
-        for shift in (64, 32, 16, 8, 4, 2, 1):
-            s = pair_add(s, tuple(pltpu.roll(v, shift, 1) for v in s))
-        away = iota(BLK, 1) - iota(BLK, 0) - 8 * n
-        line = line + jnp.where(away == 0, s[0], F32(0)) + jnp.where(away == 64, s[1], F32(0))
+    count = len(sums)
+    for k, s in enumerate(sums):
+        for n in range(2):
+            spare[n, 8 * k : 8 * k + 8, :] = s[n]
+    lines = [tuple(spare[n, pl.ds(row, count, stride=8), :] for n in range(2)) for row in range(8)]
+    while len(lines) > 1:
+        lines = [pair_add(x, y) for x, y in zip(lines[::2], lines[1::2])]
+    s = lines[0]
+    for shift in (64, 32, 16, 8, 4, 2, 1):
+        s = pair_add(s, tuple(pltpu.roll(v, shift, 1) for v in s))
+    away = iota(s[0].shape, 1) - iota(s[0].shape, 0)
+    line = jnp.where(away == 0, s[0], F32(0)) + jnp.where(away == 64, s[1], F32(0))
     line = jnp.sum(line, axis=0, keepdims=True)
     out[...] = jnp.broadcast_to(line, out.shape)
 
@@ -324,7 +321,7 @@
 def start_kernel(
     own, b2, b1, a1, a2, a3, weights, ranks, hot_z, hot_row, wave,
     p0_out, p1_out, p2_out, damp_out, gram_out,
-    field, damping, source, p0, p1,
+    field, damping, source, p0, p1, spare,
 ):
     me = lax.axis_index("space")
     for s, ref in enumerate((b2, b1, own, a1, a2, a3)):
@@ -346,13 +343,13 @@
         p0_out[k] = p0[k, 3:9]
         p1_out[k] = p1[k, 3:9]
     damp_out[...] = damping[3:9]
-    gram(((p0, 5), (p1, 5), (p2_out, 2)), PAIRS_1, gram_out)
+    gram(((p0, 5), (p1, 5), (p2_out, 2)), PAIRS_1, gram_out, spare)
 
 
 def middle_kernel(
     parts, p0, p1, p2, damping, own,
     xs_out, r_out, d_out, m_out, f_out, gram_out,
-    r, m, f, g, h,
+    r, m, f, g, h, spare,
 ):
     me = lax.axis_index("space")
     e = gathered(parts, PAIRS_1)
@@ -400,7 +397,7 @@
     apply(me, f, damping, -1, 2, 4, into(h))
     for k in range(6):
         f_out[2 * k : 2 * k + 2] = f[k, 1:3]
-    gram(((r, 2), (m, 2), (f, 2), (g, 2), (h, 2)), PAIRS_2, gram_out)
+    gram(((r, 2), (m, 2), (f, 2), (g, 2), (h, 2)), PAIRS_2, gram_out, spare)
 
 
 def end_kernel(parts, xs, r, d, m, f, background, wave, adjoint_out, terms_out):
@@ -509,7 +506,7 @@
         "start",
         [spec()] * 11,
         [six, six, six, shaped(6, *plane), shaped(n_slabs, LANES)],
-        [(6, 12, *plane), (12, *plane), (6, 12, *plane), (6, 12, *plane), (6, 12, *plane)],
+        [(6, 12, *plane), (12, *plane), *[(6, 12, *plane)] * 3, (2, 64, LANES)],
         40_000_000,
     )(message, *window, weights, *places)
     parts = lax.all_to_all(parts, "space", split_axis=0, concat_axis=0, tiled=True)
@@ -519,7 +516,7 @@
         "middle",
         [spec()] * 6,
         [two] * 5 + [shaped(n_slabs, LANES)],
-        [(6, 6, *plane)] * 5,
+        [(6, 6, *plane)] * 5 + [(2, 192, LANES)],
         40_000_000,
     )(parts, p0, p1, p2, damping, own)
     parts = lax.all_to_all(parts, "space", split_axis=0, concat_axis=0, tiled=True)

time: 72.6 us -> 72.2 us (level)
  no operation moved by 1% of the time
where the time goes in v4:
time: 72.2 us; the launch traced here: 71.9 us
  blocking collectives  37.1 us (51%)
  starting transfers between devices  15.3 us (21%)
  Pallas kernels  12.7 us (18%)
  waiting for transfers between devices  2.6 us (4%)
  other arithmetic  1.57 us (2%)
  between operations  1.38 us (2%)
  local copies, waits for them, and re-layouts  1.27 us (2%)
    all_to_all x2, blocking collectives, shards(): lax.all_to_all(parts, 'space', split_axis=0, concat_axis=0, tiled=True)  22.2 us
    all_to_all x1, blocking collectives, shards(): lax.all_to_all(terms, 'src', split_axis=0, concat_axis=0, tiled=True)  14.8 us
    ppermute x5, starting transfers between devices, from_slab(): return lax.ppermute(message, 'space', route)  9.61 us
    all_to_all x1, starting transfers between devices, shards(): lax.all_to_all(weights, 'space', split_axis=0, concat_axis=0, tiled=True)  5.74 us
    pallas_call x1, Pallas kernels, shards(): kernel(start_kernel, 'start', [spec()] * 11, [six, six, six, shaped(6, *p...  4.36 us
    pallas_call x1, Pallas kernels, shards(): kernel(middle_kernel, 'middle', [spec()] * 6, [two] * 5 + [shaped(n_slabs...  3.49 us
    pallas_call x1, Pallas kernels, shards(): kernel(functools.partial(place_kernel, n_slabs), 'place', [spec()] * 3 +...  3.37 us
    all_to_all x1, waiting for transfers between devices, shards(): lax.all_to_all(weights, 'space', split_axis=0, concat_axis=0, tiled=True)  2.59 us
  transfers between devices with their start and end apart: 6, of which 1 were waited for; matrix products, arithmetic and copies ran while one was open for 1% of the time, Pallas kernels for 5%

profile of v4, /device:TPU:1, one launch (start us, length us, event | category | flops | bytes accessed | tf_op | source)
XLA Modules:
  0.0 71.9 jit_solution(5599848796005744795)
XLA Ops:
  0.6 1.0 %pad_maximum_fusion.own = f32[14,32,128]{2,1,0:T(8,128)S(1)} fusion(f32[2,32,128]{2,1,0:T(8,128)} %param.11, f32[12,32,128]{2,1,0:T(8,128)} %bitcast.18), kind=kLoop, calls=%fused_computation | loop fusion | flops 57344 | bytes 458752 | tf_op jit(solution)/shard_map/concatenate | solution.py:474
  1.6 0.0 copy-start.6
  1.6 6.4 %collective-permute-start.4 = (f32[14,32,128]{2,1,0:T(8,128)S(1)}, f32[14,32,128]{2,1,0:T(8,128)S(1)}, u32[]{:S(2)}, u32[]{:S(2)}) collective-permute-start(f32[14,32,128]{2,1,0:T(8,128)S(1)} %pad_maximum_fusion.own), channel_id=1, source_target_pairs={{3,0},{4,1},{5,2},{6,3},{7,4},{8,5},{9,6},{10,7},{11,8},{12,9},{13... | collective-permute-start | bytes 688136 | tf_op jit(solution)/shard_map/ppermute | solution.py:478
  8.0 0.5 collective-permute-start.3
  8.5 0.6 collective-permute-start.2
  9.1 1.1 %collective-permute-start.1 = (f32[14,32,128]{2,1,0:T(8,128)S(1)}, f32[14,32,128]{2,1,0:T(8,128)S(1)}, u32[]{:S(2)}, u32[]{:S(2)}) collective-permute-start(f32[14,32,128]{2,1,0:T(8,128)S(1)} %pad_maximum_fusion.own), channel_id=1, source_target_pairs={{31,0},{0,1},{1,2},{2,3},{3,4},{4,5},{5,6},{6,7},{7,8},{8,9},{9,10... | collective-permute-start | bytes 688136 | tf_op jit(solution)/shard_map/ppermute | solution.py:478
  10.2 1.0 %collective-permute-start = (f32[14,32,128]{2,1,0:T(8,128)S(1)}, f32[14,32,128]{2,1,0:T(8,128)S(1)}, u32[]{:S(2)}, u32[]{:S(2)}) collective-permute-start(f32[14,32,128]{2,1,0:T(8,128)S(1)} %pad_maximum_fusion.own), channel_id=1, source_target_pairs={{30,0},{31,1},{0,2},{1,3},{2,4},{3,5},{4,6},{5,7},{6,8},{7,9},{8,1... | collective-permute-start | bytes 688136 | tf_op jit(solution)/shard_map/ppermute | solution.py:478
  11.2 0.0 copy-done.6
  11.2 0.6 broadcast_in_dim.8
  11.8 0.0 copy-start.2
  11.8 0.0 copy-start.3
  11.8 0.0 copy-start.4
  11.9 5.7 %all-to-all-start = ((f32[32,2,128]{2,1,0:T(2,128)}), f32[32,2,128]{2,1,0:T(2,128)S(1)}, u32[]{:S(2)}, u32[]{:S(2)}) async-start(f32[32,2,128]{2,1,0:T(2,128)} %broadcast_in_dim.8), calls=%async_computation | async-start | bytes 65536 | tf_op jit(solution)/shard_map/all_to_all | solution.py:482
  18.2 0.0 copy-start.5
  18.3 0.0 copy-done.2
  18.3 0.0 copy-done.3
  18.3 0.0 copy-done.4
  18.3 0.6 copy-done.5
  18.9 3.4 %place.1 = (f32[6,32,128]{2,1,0:T(8,128)S(1)}, f32[6,256,128]{2,1,0:T(8,128)S(1)}, bf16[6,256,256]{2,1,0:T(8,128)(2,1)S(1)}, f32[8,128]{1,0:T(8,128)S(1)}) custom-call(s32[32,128]{1,0:T(8,128)S(1)} %bitcast.25, s32[32,128]{1,0:T(8,128)S(1)} %bitcast.26, s32[32,128]{1,0:T(8,128)S(1)} %bitcast.27, f32[8]{0:T(128)S(1)} %copy-done.5, s32[1]{0:T(128)S(6)} %copy.15.pair), custom_call_target="tpu_custom_call" | custom-call | flops 20000000 | bytes 3000000 | tf_op jit(solution)/shard_map/place/pallas_call | solution.py:490
  22.3 2.6 %all-to-all-done.weights = f32[32,2,128]{2,1,0:T(2,128)S(1)} async-done(((f32[32,2,128]{2,1,0:T(2,128)}), f32[32,2,128]{2,1,0:T(2,128)S(1)}, u32[]{:S(2)}, u32[]{:S(2)}) %all-to-all-start) | async-done | bytes 32800 | tf_op jit(solution)/shard_map/all_to_all | solution.py:482
  24.9 0.0 collective-permute-done.4.a3
  24.9 0.0 collective-permute-done.3.a2
  24.9 0.0 collective-permute-done.2.a1
  24.9 0.0 collective-permute-done.1.b1
  24.9 0.0 collective-permute-done.b2
  24.9 0.0 copy-start
  24.9 4.4 %start.1 = (f32[6,6,32,128]{3,2,1,0:T(8,128)S(1)}, f32[6,6,32,128]{3,2,1,0:T(8,128)S(1)}, f32[6,6,32,128]{3,2,1,0:T(8,128)S(1)}, f32[6,32,128]{2,1,0:T(8,128)S(1)}, f32[32,128]{1,0:T(8,128)S(1)}) custom-call(f32[14,32,128]{2,1,0:T(8,128)S(1)} %pad_maximum_fusion.own, f32[14,32,128]{2,1,0:T(8,128)S(1)} %collective-permute-done.b2, ...), custom_call_target="tpu_custom_call" | custom-call | flops 40000000 | bytes 3000000 | tf_op jit(solution)/shard_map/start/pallas_call | solution.py:504
  29.3 11.6 %all_to_all.32 = f32[32,1,128]{2,1,0:T(1,128)S(1)} all-to-all(f32[32,1,128]{2,1,0:T(1,128)S(1)} %bitcast.23), channel_id=1, replica_groups=mesh['src'=8,'space'=32] {'space'}, dimensions={0} | all-to-all | bytes 32768 | tf_op jit(solution)/shard_map/all_to_all | solution.py:512
  40.8 0.0 copy-done
  40.8 0.0 copy-start.1
  40.8 3.5 %middle.1 = (f32[12,32,128]{2,1,0:T(8,128)S(1)}, f32[12,32,128]{2,1,0:T(8,128)S(1)}, f32[12,32,128]{2,1,0:T(8,128)S(1)}, f32[12,32,128]{2,1,0:T(8,128)S(1)}, f32...) custom-call(f32[32,128]{1,0:T(8,128)S(1)} %bitcast.21, f32[6,6,32,128]{3,2,1,0:T(8,128)S(1)} %get-tuple-element.24.p0, ...), custom_call_target="tpu_custom_call" | custom-call | flops 40000000 | bytes 3000000 | tf_op jit(solution)/shard_map/middle/pallas_call | solution.py:514
  44.3 10.7 %all_to_all.33 = f32[32,1,128]{2,1,0:T(1,128)S(1)} all-to-all(f32[32,1,128]{2,1,0:T(1,128)S(1)} %bitcast.24), channel_id=1, replica_groups=mesh['src'=8,'space'=32] {'space'}, dimensions={0} | all-to-all | bytes 32768 | tf_op jit(solution)/shard_map/all_to_all | solution.py:522
  55.0 0.0 copy-done.1
  55.0 1.5 %end.1 = (f32[12,32,128]{2,1,0:T(8,128)}, f32[8,8,128]{2,1,0:T(8,128)S(1)}) custom-call(f32[32,128]{1,0:T(8,128)S(1)} %bitcast.22, f32[12,32,128]{2,1,0:T(8,128)S(1)} %get-tuple-element.29.xs, f32[12,32,128]{2,1,0:T(8,128)S(1)} %get-tuple-element.30.r, f32[12,32,128]{2,1,0:T(8,128)S(1)} %get-tuple-element.31.d, f32[12,32,128]{2,1,0:T(8,128)S(1)} %get-tuple-element.32.m, ...), custom_call_target="tpu_custom_call" | custom-call | flops 5000000 | bytes 3000000 | tf_op jit(solution)/shard_map/end/pallas_call | solution.py:523
  56.5 14.8 %all_to_all.34 = f32[8,8,128]{2,1,0:T(8,128)S(1)} all-to-all(f32[8,8,128]{2,1,0:T(8,128)S(1)} %get-tuple-element.35), channel_id=1, replica_groups=mesh['src'=8,'space'=32] {'src'}, dimensions={0} | all-to-all | bytes 65536 | tf_op jit(solution)/shard_map/all_to_all | solution.py:531
  71.3 0.6 reduce_sum.9
Async XLA Ops:
  1.6 9.6 %copy-start.6 = (f32[2,1,128]{2,1,0:T(1,128)S(1)}, f32[2,1,128]{2,1,0:T(1,128)}, u32[]{:S(2)}) copy-start(f32[2,1,128]{2,1,0:T(1,128)} %param.14) | copy-start | bytes 3076
  1.6 23.3 %collective-permute-start.4 = (f32[14,32,128]{2,1,0:T(8,128)S(1)}, f32[14,32,128]{2,1,0:T(8,128)S(1)}, u32[]{:S(2)}, u32[]{:S(2)}) collective-permute-start(f32[14,32,128]{2,1,0:T(8,128)S(1)} %pad_maximum_fusion.own), channel_id=1, source_target_pairs={{3,0},{4,1},{5,2},{6,3},{7,4},{8,5},{9,6},{10,7},{11,8},{12,9},{13... | collective-permute-start | bytes 688136 | tf_op jit(solution)/shard_map/ppermute | solution.py:478
  8.0 16.9 %collective-permute-start.3 = (f32[14,32,128]{2,1,0:T(8,128)S(1)}, f32[14,32,128]{2,1,0:T(8,128)S(1)}, u32[]{:S(2)}, u32[]{:S(2)}) collective-permute-start(f32[14,32,128]{2,1,0:T(8,128)S(1)} %pad_maximum_fusion.own), channel_id=1, source_target_pairs={{2,0},{3,1},{4,2},{5,3},{6,4},{7,5},{8,6},{9,7},{10,8},{11,9},{12,... | collective-permute-start | bytes 688136 | tf_op jit(solution)/shard_map/ppermute | solution.py:478
  8.5 16.4 %collective-permute-start.2 = (f32[14,32,128]{2,1,0:T(8,128)S(1)}, f32[14,32,128]{2,1,0:T(8,128)S(1)}, u32[]{:S(2)}, u32[]{:S(2)}) collective-permute-start(f32[14,32,128]{2,1,0:T(8,128)S(1)} %pad_maximum_fusion.own), channel_id=1, source_target_pairs={{1,0},{2,1},{3,2},{4,3},{5,4},{6,5},{7,6},{8,7},{9,8},{10,9},{11,1... | collective-permute-start | bytes 688136 | tf_op jit(solution)/shard_map/ppermute | solution.py:478
  9.1 15.8 %collective-permute-start.1 = (f32[14,32,128]{2,1,0:T(8,128)S(1)}, f32[14,32,128]{2,1,0:T(8,128)S(1)}, u32[]{:S(2)}, u32[]{:S(2)}) collective-permute-start(f32[14,32,128]{2,1,0:T(8,128)S(1)} %pad_maximum_fusion.own), channel_id=1, source_target_pairs={{31,0},{0,1},{1,2},{2,3},{3,4},{4,5},{5,6},{6,7},{7,8},{8,9},{9,10... | collective-permute-start | bytes 688136 | tf_op jit(solution)/shard_map/ppermute | solution.py:478
  10.2 14.7 %collective-permute-start = (f32[14,32,128]{2,1,0:T(8,128)S(1)}, f32[14,32,128]{2,1,0:T(8,128)S(1)}, u32[]{:S(2)}, u32[]{:S(2)}) collective-permute-start(f32[14,32,128]{2,1,0:T(8,128)S(1)} %pad_maximum_fusion.own), channel_id=1, source_target_pairs={{30,0},{31,1},{0,2},{1,3},{2,4},{3,5},{4,6},{5,7},{6,8},{7,9},{8,1... | collective-permute-start | bytes 688136 | tf_op jit(solution)/shard_map/ppermute | solution.py:478
  11.8 6.4 %copy-start.2 = (s32[4096,1]{0,1:T(1,128)S(1)}, s32[4096,1]{0,1:T(1,128)}, u32[]{:S(2)}) copy-start(s32[4096,1]{0,1:T(1,128)} %param.15) | copy-start | bytes 49156
  11.8 6.4 %copy-start.3 = (s32[4096]{0:T(1024)S(1)}, s32[4096]{0:T(1024)}, u32[]{:S(2)}) copy-start(s32[4096]{0:T(1024)} %param.16) | copy-start | bytes 49156
  11.8 6.4 %copy-start.4 = (s32[4096]{0:T(1024)S(1)}, s32[4096]{0:T(1024)}, u32[]{:S(2)}) copy-start(s32[4096]{0:T(1024)} %param.17) | copy-start | bytes 49156
  11.9 13.0 %all-to-all-start = ((f32[32,2,128]{2,1,0:T(2,128)}), f32[32,2,128]{2,1,0:T(2,128)S(1)}, u32[]{:S(2)}, u32[]{:S(2)}) async-start(f32[32,2,128]{2,1,0:T(2,128)} %broadcast_in_dim.8), calls=%async_computation | async-start | bytes 65536 | tf_op jit(solution)/shard_map/all_to_all | solution.py:482
  18.2 0.7 copy-start.5
  24.9 15.9 %copy-start = (f32[2,1,3,2,32,128]{5,4,3,2,1,0:T(8,128)S(1)}, f32[2,1,3,2,32,128]{5,4,3,2,1,0:T(8,128)}, u32[]{:S(2)}) copy-start(f32[2,1,3,2,32,128]{5,4,3,2,1,0:T(8,128)} %param.10) | copy-start | bytes 589828
  40.8 14.2 %copy-start.1 = (f32[2,1,3,2,32,128]{5,4,3,2,1,0:T(8,128)S(1)}, f32[2,1,3,2,32,128]{5,4,3,2,1,0:T(8,128)}, u32[]{:S(2)}) copy-start(f32[2,1,3,2,32,128]{5,4,3,2,1,0:T(8,128)} %param.9) | copy-start | bytes 589828

commit v5 on v4

--- a/solution.py
+++ b/solution.py
@@ -257,7 +257,7 @@
     slots = n_blocks * CAP
     same = (iota((slots, slots), 0) == iota((slots, slots), 1)).astype(jnp.bfloat16)
 
-    @pl.loop(0, len(SLABS))
+    @pl.loop(0, len(SLABS), unroll=6)
     def _(s):
         slab = lax.rem(me + s + SLABS[0] + n_slabs, n_slabs)
         mine = slab_of[...] == slab

time: 72.2 us -> 71.6 us (level)
  Pallas kernels: 12.7 us -> 11.1 us
  waiting for transfers between devices: 2.6 us -> 4.16 us
    all_to_all x1, waiting for transfers between devices: 2.59 us -> 4.15 us  [shards(): lax.all_to_all(weights, 'space', split_axis=0, concat_axis=0, tiled=True)]
    pallas_call x1, Pallas kernels: 3.37 us -> 1.81 us  [shards(): kernel(functools.partial(place_kernel, n_slabs), 'place', [spec()] * 3 +...]
  transfers between devices with their start and end apart: 6 -> 6, of which waited for: 1 -> 1; matrix products, arithmetic and copies ran while one was open for 1% -> 1% of each run, Pallas kernels for 5% -> 3%
where the time goes in v5:
time: 71.6 us; the launch traced here: 71.3 us
  blocking collectives  36.5 us (51%)
  starting transfers between devices  15.3 us (21%)
  Pallas kernels  11.1 us (16%)
  waiting for transfers between devices  4.16 us (6%)
  other arithmetic  1.57 us (2%)
  between operations  1.37 us (2%)
  local copies, waits for them, and re-layouts  1.27 us (2%)
    all_to_all x2, blocking collectives, shards(): lax.all_to_all(parts, 'space', split_axis=0, concat_axis=0, tiled=True)  21.6 us
    all_to_all x1, blocking collectives, shards(): lax.all_to_all(terms, 'src', split_axis=0, concat_axis=0, tiled=True)  14.8 us
    ppermute x5, starting transfers between devices, from_slab(): return lax.ppermute(message, 'space', route)  9.61 us
    all_to_all x1, starting transfers between devices, shards(): lax.all_to_all(weights, 'space', split_axis=0, concat_axis=0, tiled=True)  5.74 us
    pallas_call x1, Pallas kernels, shards(): kernel(start_kernel, 'start', [spec()] * 11, [six, six, six, shaped(6, *p...  4.36 us
    all_to_all x1, waiting for transfers between devices, shards(): lax.all_to_all(weights, 'space', split_axis=0, concat_axis=0, tiled=True)  4.15 us
    pallas_call x1, Pallas kernels, shards(): kernel(middle_kernel, 'middle', [spec()] * 6, [two] * 5 + [shaped(n_slabs...  3.49 us
    pallas_call x1, Pallas kernels, shards(): kernel(functools.partial(place_kernel, n_slabs), 'place', [spec()] * 3 +...  1.81 us
  transfers between devices with their start and end apart: 6, of which 1 were waited for; matrix products, arithmetic and copies ran while one was open for 1% of the time, Pallas kernels for 3%

profile of v5, /device:TPU:1, one launch (start us, length us, event | category | flops | bytes accessed | tf_op | source)
XLA Modules:
  0.0 71.3 jit_solution(17173497333683806977)
XLA Ops:
  0.6 1.0 %pad_maximum_fusion.own = f32[14,32,128]{2,1,0:T(8,128)S(1)} fusion(f32[2,32,128]{2,1,0:T(8,128)} %param.11, f32[12,32,128]{2,1,0:T(8,128)} %bitcast.18), kind=kLoop, calls=%fused_computation | loop fusion | flops 57344 | bytes 458752 | tf_op jit(solution)/shard_map/concatenate | solution.py:474
  1.6 0.0 copy-start.6
  1.6 6.4 %collective-permute-start.4 = (f32[14,32,128]{2,1,0:T(8,128)S(1)}, f32[14,32,128]{2,1,0:T(8,128)S(1)}, u32[]{:S(2)}, u32[]{:S(2)}) collective-permute-start(f32[14,32,128]{2,1,0:T(8,128)S(1)} %pad_maximum_fusion.own), channel_id=1, source_target_pairs={{3,0},{4,1},{5,2},{6,3},{7,4},{8,5},{9,6},{10,7},{11,8},{12,9},{13... | collective-permute-start | bytes 688136 | tf_op jit(solution)/shard_map/ppermute | solution.py:478
  8.0 0.5 collective-permute-start.3
  8.5 0.6 collective-permute-start.2
  9.1 1.1 %collective-permute-start.1 = (f32[14,32,128]{2,1,0:T(8,128)S(1)}, f32[14,32,128]{2,1,0:T(8,128)S(1)}, u32[]{:S(2)}, u32[]{:S(2)}) collective-permute-start(f32[14,32,128]{2,1,0:T(8,128)S(1)} %pad_maximum_fusion.own), channel_id=1, source_target_pairs={{31,0},{0,1},{1,2},{2,3},{3,4},{4,5},{5,6},{6,7},{7,8},{8,9},{9,10... | collective-permute-start | bytes 688136 | tf_op jit(solution)/shard_map/ppermute | solution.py:478
  10.2 1.0 %collective-permute-start = (f32[14,32,128]{2,1,0:T(8,128)S(1)}, f32[14,32,128]{2,1,0:T(8,128)S(1)}, u32[]{:S(2)}, u32[]{:S(2)}) collective-permute-start(f32[14,32,128]{2,1,0:T(8,128)S(1)} %pad_maximum_fusion.own), channel_id=1, source_target_pairs={{30,0},{31,1},{0,2},{1,3},{2,4},{3,5},{4,6},{5,7},{6,8},{7,9},{8,1... | collective-permute-start | bytes 688136 | tf_op jit(solution)/shard_map/ppermute | solution.py:478
  11.2 0.0 copy-done.6
  11.2 0.6 broadcast_in_dim.8
  11.8 0.0 copy-start.2
  11.8 0.0 copy-start.3
  11.8 0.0 copy-start.4
  11.9 5.7 %all-to-all-start = ((f32[32,2,128]{2,1,0:T(2,128)}), f32[32,2,128]{2,1,0:T(2,128)S(1)}, u32[]{:S(2)}, u32[]{:S(2)}) async-start(f32[32,2,128]{2,1,0:T(2,128)} %broadcast_in_dim.8), calls=%async_computation | async-start | bytes 65536 | tf_op jit(solution)/shard_map/all_to_all | solution.py:482
  18.2 0.0 copy-start.5
  18.3 0.0 copy-done.2
  18.3 0.0 copy-done.3
  18.3 0.0 copy-done.4
  18.3 0.6 copy-done.5
  18.9 1.8 %place.1 = (f32[6,32,128]{2,1,0:T(8,128)S(1)}, f32[6,256,128]{2,1,0:T(8,128)S(1)}, bf16[6,256,256]{2,1,0:T(8,128)(2,1)S(1)}, f32[8,128]{1,0:T(8,128)S(1)}) custom-call(s32[32,128]{1,0:T(8,128)S(1)} %bitcast.25, s32[32,128]{1,0:T(8,128)S(1)} %bitcast.26, s32[32,128]{1,0:T(8,128)S(1)} %bitcast.27, f32[8]{0:T(128)S(1)} %copy-done.5, s32[1]{0:T(128)S(6)} %copy.15.pair), custom_call_target="tpu_custom_call" | custom-call | flops 20000000 | bytes 3000000 | tf_op jit(solution)/shard_map/place/pallas_call | solution.py:490
  20.7 4.2 %all-to-all-done.weights = f32[32,2,128]{2,1,0:T(2,128)S(1)} async-done(((f32[32,2,128]{2,1,0:T(2,128)}), f32[32,2,128]{2,1,0:T(2,128)S(1)}, u32[]{:S(2)}, u32[]{:S(2)}) %all-to-all-start) | async-done | bytes 32800 | tf_op jit(solution)/shard_map/all_to_all | solution.py:482
  24.9 0.0 collective-permute-done.4.a3
  24.9 0.0 collective-permute-done.3.a2
  24.9 0.0 collective-permute-done.2.a1
  24.9 0.0 collective-permute-done.1.b1
  24.9 0.0 collective-permute-done.b2
  24.9 0.0 copy-start
  24.9 4.4 %start.1 = (f32[6,6,32,128]{3,2,1,0:T(8,128)S(1)}, f32[6,6,32,128]{3,2,1,0:T(8,128)S(1)}, f32[6,6,32,128]{3,2,1,0:T(8,128)S(1)}, f32[6,32,128]{2,1,0:T(8,128)S(1)}, f32[32,128]{1,0:T(8,128)S(1)}) custom-call(f32[14,32,128]{2,1,0:T(8,128)S(1)} %pad_maximum_fusion.own, f32[14,32,128]{2,1,0:T(8,128)S(1)} %collective-permute-done.b2, ...), custom_call_target="tpu_custom_call" | custom-call | flops 40000000 | bytes 3000000 | tf_op jit(solution)/shard_map/start/pallas_call | solution.py:504
  29.3 11.0 %all_to_all.32 = f32[32,1,128]{2,1,0:T(1,128)S(1)} all-to-all(f32[32,1,128]{2,1,0:T(1,128)S(1)} %bitcast.23), channel_id=1, replica_groups=mesh['src'=8,'space'=32] {'space'}, dimensions={0} | all-to-all | bytes 32768 | tf_op jit(solution)/shard_map/all_to_all | solution.py:512
  40.2 0.0 copy-done
  40.2 0.0 copy-start.1
  40.2 3.5 %middle.1 = (f32[12,32,128]{2,1,0:T(8,128)S(1)}, f32[12,32,128]{2,1,0:T(8,128)S(1)}, f32[12,32,128]{2,1,0:T(8,128)S(1)}, f32[12,32,128]{2,1,0:T(8,128)S(1)}, f32...) custom-call(f32[32,128]{1,0:T(8,128)S(1)} %bitcast.21, f32[6,6,32,128]{3,2,1,0:T(8,128)S(1)} %get-tuple-element.24.p0, ...), custom_call_target="tpu_custom_call" | custom-call | flops 40000000 | bytes 3000000 | tf_op jit(solution)/shard_map/middle/pallas_call | solution.py:514
  43.7 10.7 %all_to_all.33 = f32[32,1,128]{2,1,0:T(1,128)S(1)} all-to-all(f32[32,1,128]{2,1,0:T(1,128)S(1)} %bitcast.24), channel_id=1, replica_groups=mesh['src'=8,'space'=32] {'space'}, dimensions={0} | all-to-all | bytes 32768 | tf_op jit(solution)/shard_map/all_to_all | solution.py:522
  54.4 0.0 copy-done.1
  54.4 1.5 %end.1 = (f32[12,32,128]{2,1,0:T(8,128)}, f32[8,8,128]{2,1,0:T(8,128)S(1)}) custom-call(f32[32,128]{1,0:T(8,128)S(1)} %bitcast.22, f32[12,32,128]{2,1,0:T(8,128)S(1)} %get-tuple-element.29.xs, f32[12,32,128]{2,1,0:T(8,128)S(1)} %get-tuple-element.30.r, f32[12,32,128]{2,1,0:T(8,128)S(1)} %get-tuple-element.31.d, f32[12,32,128]{2,1,0:T(8,128)S(1)} %get-tuple-element.32.m, ...), custom_call_target="tpu_custom_call" | custom-call | flops 5000000 | bytes 3000000 | tf_op jit(solution)/shard_map/end/pallas_call | solution.py:523
  55.9 14.8 %all_to_all.34 = f32[8,8,128]{2,1,0:T(8,128)S(1)} all-to-all(f32[8,8,128]{2,1,0:T(8,128)S(1)} %get-tuple-element.35), channel_id=1, replica_groups=mesh['src'=8,'space'=32] {'src'}, dimensions={0} | all-to-all | bytes 65536 | tf_op jit(solution)/shard_map/all_to_all | solution.py:531
  70.7 0.6 reduce_sum.9
Async XLA Ops:
  1.6 9.6 %copy-start.6 = (f32[2,1,128]{2,1,0:T(1,128)S(1)}, f32[2,1,128]{2,1,0:T(1,128)}, u32[]{:S(2)}) copy-start(f32[2,1,128]{2,1,0:T(1,128)} %param.14) | copy-start | bytes 3076
  1.6 23.3 %collective-permute-start.4 = (f32[14,32,128]{2,1,0:T(8,128)S(1)}, f32[14,32,128]{2,1,0:T(8,128)S(1)}, u32[]{:S(2)}, u32[]{:S(2)}) collective-permute-start(f32[14,32,128]{2,1,0:T(8,128)S(1)} %pad_maximum_fusion.own), channel_id=1, source_target_pairs={{3,0},{4,1},{5,2},{6,3},{7,4},{8,5},{9,6},{10,7},{11,8},{12,9},{13... | collective-permute-start | bytes 688136 | tf_op jit(solution)/shard_map/ppermute | solution.py:478
  8.0 16.9 %collective-permute-start.3 = (f32[14,32,128]{2,1,0:T(8,128)S(1)}, f32[14,32,128]{2,1,0:T(8,128)S(1)}, u32[]{:S(2)}, u32[]{:S(2)}) collective-permute-start(f32[14,32,128]{2,1,0:T(8,128)S(1)} %pad_maximum_fusion.own), channel_id=1, source_target_pairs={{2,0},{3,1},{4,2},{5,3},{6,4},{7,5},{8,6},{9,7},{10,8},{11,9},{12,... | collective-permute-start | bytes 688136 | tf_op jit(solution)/shard_map/ppermute | solution.py:478
  8.5 16.4 %collective-permute-start.2 = (f32[14,32,128]{2,1,0:T(8,128)S(1)}, f32[14,32,128]{2,1,0:T(8,128)S(1)}, u32[]{:S(2)}, u32[]{:S(2)}) collective-permute-start(f32[14,32,128]{2,1,0:T(8,128)S(1)} %pad_maximum_fusion.own), channel_id=1, source_target_pairs={{1,0},{2,1},{3,2},{4,3},{5,4},{6,5},{7,6},{8,7},{9,8},{10,9},{11,1... | collective-permute-start | bytes 688136 | tf_op jit(solution)/shard_map/ppermute | solution.py:478
  9.1 15.8 %collective-permute-start.1 = (f32[14,32,128]{2,1,0:T(8,128)S(1)}, f32[14,32,128]{2,1,0:T(8,128)S(1)}, u32[]{:S(2)}, u32[]{:S(2)}) collective-permute-start(f32[14,32,128]{2,1,0:T(8,128)S(1)} %pad_maximum_fusion.own), channel_id=1, source_target_pairs={{31,0},{0,1},{1,2},{2,3},{3,4},{4,5},{5,6},{6,7},{7,8},{8,9},{9,10... | collective-permute-start | bytes 688136 | tf_op jit(solution)/shard_map/ppermute | solution.py:478
  10.2 14.7 %collective-permute-start = (f32[14,32,128]{2,1,0:T(8,128)S(1)}, f32[14,32,128]{2,1,0:T(8,128)S(1)}, u32[]{:S(2)}, u32[]{:S(2)}) collective-permute-start(f32[14,32,128]{2,1,0:T(8,128)S(1)} %pad_maximum_fusion.own), channel_id=1, source_target_pairs={{30,0},{31,1},{0,2},{1,3},{2,4},{3,5},{4,6},{5,7},{6,8},{7,9},{8,1... | collective-permute-start | bytes 688136 | tf_op jit(solution)/shard_map/ppermute | solution.py:478
  11.8 6.4 %copy-start.2 = (s32[4096,1]{0,1:T(1,128)S(1)}, s32[4096,1]{0,1:T(1,128)}, u32[]{:S(2)}) copy-start(s32[4096,1]{0,1:T(1,128)} %param.15) | copy-start | bytes 49156
  11.8 6.4 %copy-start.3 = (s32[4096]{0:T(1024)S(1)}, s32[4096]{0:T(1024)}, u32[]{:S(2)}) copy-start(s32[4096]{0:T(1024)} %param.16) | copy-start | bytes 49156
  11.8 6.4 %copy-start.4 = (s32[4096]{0:T(1024)S(1)}, s32[4096]{0:T(1024)}, u32[]{:S(2)}) copy-start(s32[4096]{0:T(1024)} %param.17) | copy-start | bytes 49156
  11.9 13.0 %all-to-all-start = ((f32[32,2,128]{2,1,0:T(2,128)}), f32[32,2,128]{2,1,0:T(2,128)S(1)}, u32[]{:S(2)}, u32[]{:S(2)}) async-start(f32[32,2,128]{2,1,0:T(2,128)} %broadcast_in_dim.8), calls=%async_computation | async-start | bytes 65536 | tf_op jit(solution)/shard_map/all_to_all | solution.py:482
  18.2 0.7 copy-start.5
  24.9 15.3 %copy-start = (f32[2,1,3,2,32,128]{5,4,3,2,1,0:T(8,128)S(1)}, f32[2,1,3,2,32,128]{5,4,3,2,1,0:T(8,128)}, u32[]{:S(2)}) copy-start(f32[2,1,3,2,32,128]{5,4,3,2,1,0:T(8,128)} %param.10) | copy-start | bytes 589828
  40.2 14.2 %copy-start.1 = (f32[2,1,3,2,32,128]{5,4,3,2,1,0:T(8,128)S(1)}, f32[2,1,3,2,32,128]{5,4,3,2,1,0:T(8,128)}, u32[]{:S(2)}) copy-start(f32[2,1,3,2,32,128]{5,4,3,2,1,0:T(8,128)} %param.9) | copy-start | bytes 589828

commit v6 on v5

--- a/solution.py
+++ b/solution.py
@@ -59,7 +59,10 @@
 
 
 def total(terms):
-    return functools.reduce(pair_add, terms)
+    terms = list(terms)
+    while len(terms) > 1:
+        terms = [pair_add(x, y) for x, y in zip(terms[::2], terms[1::2])] + terms[len(terms) // 2 * 2 :]
+    return terms[0]
 
 
 def mix_re(g, v):
@@ -367,7 +370,7 @@
     v = cmul(step, a)
     a, u, s, v = rows(a), rows(u), rows(s), rows(v)
 
-    @pl.loop(0, 6)
+    @pl.loop(0, 6, unroll=3)
     def _(at):
         for c in range(3):
             v0 = (p0[c, at], p0[3 + c, at])

time: 71.6 us -> 71.6 us (level)
  no operation moved by 1% of the time
where the time goes in v6:
time: 71.6 us; the launch traced here: 71.3 us
  blocking collectives  36.5 us (51%)
  starting transfers between devices  15.3 us (21%)
  Pallas kernels  11.1 us (16%)
  waiting for transfers between devices  4.16 us (6%)
  other arithmetic  1.57 us (2%)
  between operations  1.37 us (2%)
  local copies, waits for them, and re-layouts  1.27 us (2%)
    all_to_all x2, blocking collectives, shards(): lax.all_to_all(parts, 'space', split_axis=0, concat_axis=0, tiled=True)  21.6 us
    all_to_all x1, blocking collectives, shards(): lax.all_to_all(terms, 'src', split_axis=0, concat_axis=0, tiled=True)  14.8 us
    ppermute x5, starting transfers between devices, from_slab(): return lax.ppermute(message, 'space', route)  9.61 us
    all_to_all x1, starting transfers between devices, shards(): lax.all_to_all(weights, 'space', split_axis=0, concat_axis=0, tiled=True)  5.74 us
    pallas_call x1, Pallas kernels, shards(): kernel(start_kernel, 'start', [spec()] * 11, [six, six, six, shaped(6, *p...  4.36 us
    all_to_all x1, waiting for transfers between devices, shards(): lax.all_to_all(weights, 'space', split_axis=0, concat_axis=0, tiled=True)  4.15 us
    pallas_call x1, Pallas kernels, shards(): kernel(middle_kernel, 'middle', [spec()] * 6, [two] * 5 + [shaped(n_slabs...  3.46 us
    pallas_call x1, Pallas kernels, shards(): kernel(functools.partial(place_kernel, n_slabs), 'place', [spec()] * 3 +...  1.81 us
  transfers between devices with their start and end apart: 6, of which 1 were waited for; matrix products, arithmetic and copies ran while one was open for 1% of the time, Pallas kernels for 3%

profile of v6, /device:TPU:1, one launch (start us, length us, event | category | flops | bytes accessed | tf_op | source)
XLA Modules:
  0.0 71.3 jit_solution(13621694435721465597)
XLA Ops:
  0.6 1.0 %pad_maximum_fusion.own = f32[14,32,128]{2,1,0:T(8,128)S(1)} fusion(f32[2,32,128]{2,1,0:T(8,128)} %param.11, f32[12,32,128]{2,1,0:T(8,128)} %bitcast.18), kind=kLoop, calls=%fused_computation | loop fusion | flops 57344 | bytes 458752 | tf_op jit(solution)/shard_map/concatenate | solution.py:477
  1.6 0.0 copy-start.6
  1.6 6.4 %collective-permute-start.4 = (f32[14,32,128]{2,1,0:T(8,128)S(1)}, f32[14,32,128]{2,1,0:T(8,128)S(1)}, u32[]{:S(2)}, u32[]{:S(2)}) collective-permute-start(f32[14,32,128]{2,1,0:T(8,128)S(1)} %pad_maximum_fusion.own), channel_id=1, source_target_pairs={{3,0},{4,1},{5,2},{6,3},{7,4},{8,5},{9,6},{10,7},{11,8},{12,9},{13... | collective-permute-start | bytes 688136 | tf_op jit(solution)/shard_map/ppermute | solution.py:481
  8.0 0.5 collective-permute-start.3
  8.5 0.6 collective-permute-start.2
  9.1 1.1 %collective-permute-start.1 = (f32[14,32,128]{2,1,0:T(8,128)S(1)}, f32[14,32,128]{2,1,0:T(8,128)S(1)}, u32[]{:S(2)}, u32[]{:S(2)}) collective-permute-start(f32[14,32,128]{2,1,0:T(8,128)S(1)} %pad_maximum_fusion.own), channel_id=1, source_target_pairs={{31,0},{0,1},{1,2},{2,3},{3,4},{4,5},{5,6},{6,7},{7,8},{8,9},{9,10... | collective-permute-start | bytes 688136 | tf_op jit(solution)/shard_map/ppermute | solution.py:481
  10.2 1.0 %collective-permute-start = (f32[14,32,128]{2,1,0:T(8,128)S(1)}, f32[14,32,128]{2,1,0:T(8,128)S(1)}, u32[]{:S(2)}, u32[]{:S(2)}) collective-permute-start(f32[14,32,128]{2,1,0:T(8,128)S(1)} %pad_maximum_fusion.own), channel_id=1, source_target_pairs={{30,0},{31,1},{0,2},{1,3},{2,4},{3,5},{4,6},{5,7},{6,8},{7,9},{8,1... | collective-permute-start | bytes 688136 | tf_op jit(solution)/shard_map/ppermute | solution.py:481
  11.2 0.0 copy-done.6
  11.2 0.6 broadcast_in_dim.8
  11.8 0.0 copy-start.2
  11.8 0.0 copy-start.3
  11.8 0.0 copy-start.4
  11.9 5.7 %all-to-all-start = ((f32[32,2,128]{2,1,0:T(2,128)}), f32[32,2,128]{2,1,0:T(2,128)S(1)}, u32[]{:S(2)}, u32[]{:S(2)}) async-start(f32[32,2,128]{2,1,0:T(2,128)} %broadcast_in_dim.8), calls=%async_computation | async-start | bytes 65536 | tf_op jit(solution)/shard_map/all_to_all | solution.py:485
  18.2 0.0 copy-start.5
  18.3 0.0 copy-done.2
  18.3 0.0 copy-done.3
  18.3 0.0 copy-done.4
  18.3 0.6 copy-done.5
  18.9 1.8 %place.1 = (f32[6,32,128]{2,1,0:T(8,128)S(1)}, f32[6,256,128]{2,1,0:T(8,128)S(1)}, bf16[6,256,256]{2,1,0:T(8,128)(2,1)S(1)}, f32[8,128]{1,0:T(8,128)S(1)}) custom-call(s32[32,128]{1,0:T(8,128)S(1)} %bitcast.25, s32[32,128]{1,0:T(8,128)S(1)} %bitcast.26, s32[32,128]{1,0:T(8,128)S(1)} %bitcast.27, f32[8]{0:T(128)S(1)} %copy-done.5, s32[1]{0:T(128)S(6)} %copy.15.pair), custom_call_target="tpu_custom_call" | custom-call | flops 20000000 | bytes 3000000 | tf_op jit(solution)/shard_map/place/pallas_call | solution.py:493
  20.7 4.2 %all-to-all-done.weights = f32[32,2,128]{2,1,0:T(2,128)S(1)} async-done(((f32[32,2,128]{2,1,0:T(2,128)}), f32[32,2,128]{2,1,0:T(2,128)S(1)}, u32[]{:S(2)}, u32[]{:S(2)}) %all-to-all-start) | async-done | bytes 32800 | tf_op jit(solution)/shard_map/all_to_all | solution.py:485
  24.9 0.0 collective-permute-done.4.a3
  24.9 0.0 collective-permute-done.3.a2
  24.9 0.0 collective-permute-done.2.a1
  24.9 0.0 collective-permute-done.1.b1
  24.9 0.0 collective-permute-done.b2
  24.9 0.0 copy-start
  24.9 4.4 %start.1 = (f32[6,6,32,128]{3,2,1,0:T(8,128)S(1)}, f32[6,6,32,128]{3,2,1,0:T(8,128)S(1)}, f32[6,6,32,128]{3,2,1,0:T(8,128)S(1)}, f32[6,32,128]{2,1,0:T(8,128)S(1)}, f32[32,128]{1,0:T(8,128)S(1)}) custom-call(f32[14,32,128]{2,1,0:T(8,128)S(1)} %pad_maximum_fusion.own, f32[14,32,128]{2,1,0:T(8,128)S(1)} %collective-permute-done.b2, ...), custom_call_target="tpu_custom_call" | custom-call | flops 40000000 | bytes 3000000 | tf_op jit(solution)/shard_map/start/pallas_call | solution.py:507
  29.3 11.0 %all_to_all.32 = f32[32,1,128]{2,1,0:T(1,128)S(1)} all-to-all(f32[32,1,128]{2,1,0:T(1,128)S(1)} %bitcast.23), channel_id=1, replica_groups=mesh['src'=8,'space'=32] {'space'}, dimensions={0} | all-to-all | bytes 32768 | tf_op jit(solution)/shard_map/all_to_all | solution.py:515
  40.2 0.0 copy-done
  40.2 0.0 copy-start.1
  40.2 3.5 %middle.1 = (f32[12,32,128]{2,1,0:T(8,128)S(1)}, f32[12,32,128]{2,1,0:T(8,128)S(1)}, f32[12,32,128]{2,1,0:T(8,128)S(1)}, f32[12,32,128]{2,1,0:T(8,128)S(1)}, f32...) custom-call(f32[32,128]{1,0:T(8,128)S(1)} %bitcast.21, f32[6,6,32,128]{3,2,1,0:T(8,128)S(1)} %get-tuple-element.24.p0, ...), custom_call_target="tpu_custom_call" | custom-call | flops 40000000 | bytes 3000000 | tf_op jit(solution)/shard_map/middle/pallas_call | solution.py:517
  43.7 10.7 %all_to_all.33 = f32[32,1,128]{2,1,0:T(1,128)S(1)} all-to-all(f32[32,1,128]{2,1,0:T(1,128)S(1)} %bitcast.24), channel_id=1, replica_groups=mesh['src'=8,'space'=32] {'space'}, dimensions={0} | all-to-all | bytes 32768 | tf_op jit(solution)/shard_map/all_to_all | solution.py:525
  54.4 0.0 copy-done.1
  54.4 1.5 %end.1 = (f32[12,32,128]{2,1,0:T(8,128)}, f32[8,8,128]{2,1,0:T(8,128)S(1)}) custom-call(f32[32,128]{1,0:T(8,128)S(1)} %bitcast.22, f32[12,32,128]{2,1,0:T(8,128)S(1)} %get-tuple-element.29.xs, f32[12,32,128]{2,1,0:T(8,128)S(1)} %get-tuple-element.30.r, f32[12,32,128]{2,1,0:T(8,128)S(1)} %get-tuple-element.31.d, f32[12,32,128]{2,1,0:T(8,128)S(1)} %get-tuple-element.32.m, ...), custom_call_target="tpu_custom_call" | custom-call | flops 5000000 | bytes 3000000 | tf_op jit(solution)/shard_map/end/pallas_call | solution.py:526
  55.8 14.8 %all_to_all.34 = f32[8,8,128]{2,1,0:T(8,128)S(1)} all-to-all(f32[8,8,128]{2,1,0:T(8,128)S(1)} %get-tuple-element.35), channel_id=1, replica_groups=mesh['src'=8,'space'=32] {'src'}, dimensions={0} | all-to-all | bytes 65536 | tf_op jit(solution)/shard_map/all_to_all | solution.py:534
  70.7 0.6 reduce_sum.9
Async XLA Ops:
  1.6 9.6 %copy-start.6 = (f32[2,1,128]{2,1,0:T(1,128)S(1)}, f32[2,1,128]{2,1,0:T(1,128)}, u32[]{:S(2)}) copy-start(f32[2,1,128]{2,1,0:T(1,128)} %param.14) | copy-start | bytes 3076
  1.6 23.3 %collective-permute-start.4 = (f32[14,32,128]{2,1,0:T(8,128)S(1)}, f32[14,32,128]{2,1,0:T(8,128)S(1)}, u32[]{:S(2)}, u32[]{:S(2)}) collective-permute-start(f32[14,32,128]{2,1,0:T(8,128)S(1)} %pad_maximum_fusion.own), channel_id=1, source_target_pairs={{3,0},{4,1},{5,2},{6,3},{7,4},{8,5},{9,6},{10,7},{11,8},{12,9},{13... | collective-permute-start | bytes 688136 | tf_op jit(solution)/shard_map/ppermute | solution.py:481
  8.0 16.9 %collective-permute-start.3 = (f32[14,32,128]{2,1,0:T(8,128)S(1)}, f32[14,32,128]{2,1,0:T(8,128)S(1)}, u32[]{:S(2)}, u32[]{:S(2)}) collective-permute-start(f32[14,32,128]{2,1,0:T(8,128)S(1)} %pad_maximum_fusion.own), channel_id=1, source_target_pairs={{2,0},{3,1},{4,2},{5,3},{6,4},{7,5},{8,6},{9,7},{10,8},{11,9},{12,... | collective-permute-start | bytes 688136 | tf_op jit(solution)/shard_map/ppermute | solution.py:481
  8.5 16.4 %collective-permute-start.2 = (f32[14,32,128]{2,1,0:T(8,128)S(1)}, f32[14,32,128]{2,1,0:T(8,128)S(1)}, u32[]{:S(2)}, u32[]{:S(2)}) collective-permute-start(f32[14,32,128]{2,1,0:T(8,128)S(1)} %pad_maximum_fusion.own), channel_id=1, source_target_pairs={{1,0},{2,1},{3,2},{4,3},{5,4},{6,5},{7,6},{8,7},{9,8},{10,9},{11,1... | collective-permute-start | bytes 688136 | tf_op jit(solution)/shard_map/ppermute | solution.py:481
  9.1 15.8 %collective-permute-start.1 = (f32[14,32,128]{2,1,0:T(8,128)S(1)}, f32[14,32,128]{2,1,0:T(8,128)S(1)}, u32[]{:S(2)}, u32[]{:S(2)}) collective-permute-start(f32[14,32,128]{2,1,0:T(8,128)S(1)} %pad_maximum_fusion.own), channel_id=1, source_target_pairs={{31,0},{0,1},{1,2},{2,3},{3,4},{4,5},{5,6},{6,7},{7,8},{8,9},{9,10... | collective-permute-start | bytes 688136 | tf_op jit(solution)/shard_map/ppermute | solution.py:481
  10.2 14.7 %collective-permute-start = (f32[14,32,128]{2,1,0:T(8,128)S(1)}, f32[14,32,128]{2,1,0:T(8,128)S(1)}, u32[]{:S(2)}, u32[]{:S(2)}) collective-permute-start(f32[14,32,128]{2,1,0:T(8,128)S(1)} %pad_maximum_fusion.own), channel_id=1, source_target_pairs={{30,0},{31,1},{0,2},{1,3},{2,4},{3,5},{4,6},{5,7},{6,8},{7,9},{8,1... | collective-permute-start | bytes 688136 | tf_op jit(solution)/shard_map/ppermute | solution.py:481
  11.8 6.4 %copy-start.2 = (s32[4096,1]{0,1:T(1,128)S(1)}, s32[4096,1]{0,1:T(1,128)}, u32[]{:S(2)}) copy-start(s32[4096,1]{0,1:T(1,128)} %param.15) | copy-start | bytes 49156
  11.8 6.4 %copy-start.3 = (s32[4096]{0:T(1024)S(1)}, s32[4096]{0:T(1024)}, u32[]{:S(2)}) copy-start(s32[4096]{0:T(1024)} %param.16) | copy-start | bytes 49156
  11.8 6.4 %copy-start.4 = (s32[4096]{0:T(1024)S(1)}, s32[4096]{0:T(1024)}, u32[]{:S(2)}) copy-start(s32[4096]{0:T(1024)} %param.17) | copy-start | bytes 49156
  11.9 13.0 %all-to-all-start = ((f32[32,2,128]{2,1,0:T(2,128)}), f32[32,2,128]{2,1,0:T(2,128)S(1)}, u32[]{:S(2)}, u32[]{:S(2)}) async-start(f32[32,2,128]{2,1,0:T(2,128)} %broadcast_in_dim.8), calls=%async_computation | async-start | bytes 65536 | tf_op jit(solution)/shard_map/all_to_all | solution.py:485
  18.2 0.7 copy-start.5
  24.9 15.3 %copy-start = (f32[2,1,3,2,32,128]{5,4,3,2,1,0:T(8,128)S(1)}, f32[2,1,3,2,32,128]{5,4,3,2,1,0:T(8,128)}, u32[]{:S(2)}) copy-start(f32[2,1,3,2,32,128]{5,4,3,2,1,0:T(8,128)} %param.10) | copy-start | bytes 589828
  40.2 14.1 %copy-start.1 = (f32[2,1,3,2,32,128]{5,4,3,2,1,0:T(8,128)S(1)}, f32[2,1,3,2,32,128]{5,4,3,2,1,0:T(8,128)}, u32[]{:S(2)}) copy-start(f32[2,1,3,2,32,128]{5,4,3,2,1,0:T(8,128)} %param.9) | copy-start | bytes 589828
